TPU v7x, 32 devices: a whole 2x2x4 slice. The times are simulated.
32 devices in a mesh: gx: 4 (over x, core), gy: 8 (over z, y).
Axes of the slice: x: 2, y: 2, z: 4, core: 2. Of those that a mesh axis runs over, the one named last changes fastest.
Arguments:
- velocity_section: float32 [3, 64, 64, 1024], P(None, 'gx', None, 'gy')
- point_owner: int32 [4, 240], P('gx'), may hold values from 0 to 7
- point_cell: int32 [4, 3, 240], P('gx'), may hold values from 0 to 127, as said below
- blade_coef: float32 [4, 240], P('gx'), may hold values from 0.5 to 2
- recycle_map: int32 [8], replicated, may hold values from 0 to 7, as said below
Outputs:
- rate: float32 [3, 64, 64, 1024], P(None, 'gx', None, 'gy')
- spread: float32 [3, 64, 64, 1024], P(None, 'gx', None, 'gy')
- point_force: float32 [4, 3, 240], P('gx')
Inputs may be any that keep to these rules, and one draw needn't show every extreme that they name: `point_cell`: row 0 is below 16, row 1 below 128, row 2 below 64. `recycle_map`: a permutation of the spanwise blocks.
All inputs are finite; a program needn't handle non-finite values.
Results may differ from a plain program's by a relative error of at most 0.0022.
Values sent between devices are 32-bit elements; how exact they have to be, the bound alone decides.
A program may use at most 192 MiB of HBM per device.

v0:
```python
import math

import jax
import jax.numpy as jnp
from jax import lax
from jax.sharding import PartitionSpec as P

BLADES = 3
BLADE_PTS = 40


viscosity = 0.02
smag_sq = 0.0256
kernel_sq = 4.0
kernel_reach = 4
force_gain = 4.0
fringe_base = 0.05
fringe_ramp = 0.45
kernel_norm = 1.0 / math.sqrt(math.pi * kernel_sq)


def broadcast(block, axis, holder):
    block = jnp.where(lax.axis_index(axis) == holder, block, jnp.zeros_like(block))
    return lax.psum(block, axis)


def padded_2(cells, sides, width):
    for axis, dim in sides:
        count = lax.axis_size(axis)
        head = lax.slice_in_dim(cells, 0, width, axis=dim)
        tail = lax.slice_in_dim(cells, cells.shape[dim] - width, cells.shape[dim], axis=dim)
        cells = jnp.concatenate(
            [
                lax.ppermute(tail, axis, [(i, (i + 1) % count) for i in range(count)]),
                cells,
                lax.ppermute(head, axis, [((i + 1) % count, i) for i in range(count)]),
            ],
            axis=dim,
        )
    return cells


def kernel_weight(distance):
    inside = jnp.abs(distance) <= kernel_reach
    return jnp.where(inside, jnp.exp(-(distance * distance) / kernel_sq) * kernel_norm, 0.0)


def tendency(padded):
    center = padded[:, 1:-1, 1:-1, 1:-1]
    x_plus = padded[:, 2:, 1:-1, 1:-1]
    x_minus = padded[:, :-2, 1:-1, 1:-1]
    z_plus = padded[:, 1:-1, 2:, 1:-1]
    z_minus = padded[:, 1:-1, :-2, 1:-1]
    y_plus = padded[:, 1:-1, 1:-1, 2:]
    y_minus = padded[:, 1:-1, 1:-1, :-2]
    gradients = [(x_plus - x_minus) * 0.5, (y_plus - y_minus) * 0.5, (z_plus - z_minus) * 0.5]
    advect = center[0] * gradients[0] + center[1] * gradients[1] + center[2] * gradients[2]
    strain = jnp.zeros_like(center[0])
    for comp_a in range(3):
        for comp_b in range(3):
            shear = 0.5 * (gradients[comp_b][comp_a] + gradients[comp_a][comp_b])
            strain = strain + shear * shear
    eddy_visc = viscosity + smag_sq * jnp.sqrt(2.0 * strain)
    laplace = x_plus + x_minus + y_plus + y_minus + z_plus + z_minus - 6.0 * center
    return (center, eddy_visc * laplace - advect)


def point_forces(values, blade_gain):
    per_turb = BLADES * BLADE_PTS
    axial_mean = jnp.mean(values[0].reshape(-1, per_turb), axis=1)
    axial_rows = jnp.repeat(axial_mean * axial_mean, per_turb)
    speeds = jnp.sqrt(jnp.sum(values * values, axis=0))
    thrust = jnp.concatenate([axial_rows[None], jnp.zeros_like(values[1:])], 0)
    return -force_gain * blade_gain[None] * (speeds[None] * values + thrust)


def local(velocity_section, point_owner, point_cell, blade_coef, recycle_map):
    cells_x = velocity_section.shape[1]
    levels = velocity_section.shape[2]
    cells_y = velocity_section.shape[3]
    count_x = lax.axis_size("gx")
    count_y = lax.axis_size("gy")
    column_id = lax.axis_index("gx")
    span_id = lax.axis_index("gy")
    source_col = 3 * count_x // 4
    owners = point_owner[0]
    cells = point_cell[0]
    blade_gain = blade_coef[0]
    loc_x = cells[0]
    loc_y = cells[1]
    levels_at = cells[2]
    at_points = velocity_section[:, loc_x, levels_at, loc_y]
    partial_value = jnp.where((owners == span_id)[None], at_points, 0.0)
    own_plane = velocity_section[:, 0]
    gathered = lax.all_gather(own_plane, "gy", axis=2, tiled=True)
    values = lax.psum(partial_value, "gy")
    gathered, values = (gathered, values)
    chosen = lax.dynamic_slice_in_dim(gathered, recycle_map[span_id] * cells_y, cells_y, 2)
    inflow = broadcast(chosen, "gx", source_col)
    forces = point_forces(values, blade_gain)
    padded = padded_2(velocity_section, (("gx", 1), ("gy", 3)), 1)
    below = jnp.where(column_id == 0, jnp.pad(inflow, ((0, 0), (0, 0), (1, 1))), padded[:, 0])
    above = jnp.where(
        column_id == count_x - 1,
        jnp.pad(velocity_section[:, -1], ((0, 0), (0, 0), (1, 1))),
        padded[:, -1],
    )
    extended = jnp.concatenate([below[:, None], padded[:, 1:-1], above[:, None]], 1)
    extended = jnp.pad(extended, ((0, 0), (0, 0), (1, 1), (0, 0)))
    center, tendency_core = tendency(extended)
    x_glob = (column_id * cells_x + jnp.arange(cells_x, dtype=jnp.int32)).astype(jnp.float32)
    fringe = fringe_base + fringe_ramp * (x_glob + 0.5) / (count_x * cells_x)
    tendency_core = tendency_core - fringe[None, :, None, None] * (center - inflow[:, None])
    x_cells = jnp.arange(cells_x, dtype=jnp.int32)
    z_cells = jnp.arange(levels, dtype=jnp.int32)
    y_cells = span_id * cells_y + jnp.arange(cells_y, dtype=jnp.int32)
    span_total = count_y * cells_y
    glob_y = owners * cells_y + loc_y
    weight_x = kernel_weight((x_cells[None, :] - loc_x[:, None]).astype(jnp.float32))
    weight_z = kernel_weight((z_cells[None, :] - levels_at[:, None]).astype(jnp.float32))
    distance = (
        jnp.mod(y_cells[None, :] - glob_y[:, None] + span_total // 2, span_total) - span_total // 2
    )
    weight_y = kernel_weight(distance.astype(jnp.float32)).astype(jnp.bfloat16)
    blocks = cells_x // 4
    weight_blocks = weight_x.reshape(-1, blocks, 4).transpose(1, 2, 0)
    weight_levels = weight_z.T

    def spread_block(block_weight):
        weighted = (
            forces[:, None, None, :]
            * block_weight[None, :, None, :]
            * weight_levels[None, None, :, :]
        ).astype(jnp.bfloat16)
        flattened = weighted.reshape(3 * 4 * levels, -1)
        return jnp.dot(flattened, weight_y, preferred_element_type=jnp.float32).reshape(
            3, 4, levels, cells_y
        )

    spread_field = lax.map(spread_block, weight_blocks)
    spread_field = spread_field.transpose(1, 0, 2, 3, 4).reshape(3, cells_x, levels, cells_y)
    return (tendency_core, spread_field, forces[None])


def solution(mesh):
    placed = (P(None, "gx", None, "gy"), P("gx", None), P("gx", None, None), P("gx", None), P())
    return jax.shard_map(
        local,
        mesh=mesh,
        in_specs=placed,
        out_specs=(P(None, "gx", None, "gy"), P(None, "gx", None, "gy"), P("gx", None, None)),
        check_vma=False,
    )
```

profile of v0, /device:TPU:0, one launch (start us, length us, event | category | flops | bytes accessed | tf_op | source)
XLA Modules:
  0.0 204.6 jit_solution(1958018737814018974)
XLA Ops:
  9.0 2.4 %collective-permute-start.1 = (f32[3,1,64,128]{2,3,0,1:T(8,128)}, f32[3,1,64,128]{2,3,0,1:T(8,128)S(1)}, u32[]{:S(2)}, u32[]{:S(2)}) collective-permute-start(f32[3,1,64,128]{2,3,0,1:T(8,128)} %copy.64), channel_id=1, source_target_pairs={{8,0},{16,8},{24,16},{0,24},{9,1},{17,9},{25,17},{1,25},{10,2},{18... | collective-permute-start | bytes 294920 | tf_op jit(solution)/shard_map/ppermute | solution.py:36
  11.4 38.1 %all-gather = f32[3,1,64,1024]{2,3,0,1:T(8,128)S(1)} all-gather(f32[3,1,64,128]{2,3,0,1:T(8,128)} %copy.64), channel_id=2, replica_groups=mesh['gx'=4,'gy'=8] {'gy'}, dimensions={3}, use_global_device_ids=true | all-gather | bytes 884736 | tf_op jit(solution)/shard_map/all_gather | solution.py:95
  53.0 2.1 %copy.42 = f32[3,16,64,128]{2,3,1,0:T(8,128)S(1)} copy(f32[3,16,64,128]{3,2,1,0:T(8,128)} %param.7) | data formatting | bytes 3145728 | tf_op args[0]
  55.1 33.2 %copy.55 = f32[3,16,64,128]{0,3,2,1:T(8,128)} copy(f32[3,16,64,128]{3,2,1,0:T(8,128)} %param.7) | data formatting | bytes 3145728 | tf_op args[0]
  88.3 4.3 %gather_fusion = f32[240,3]{1,0:T(8,128)} fusion(f32[3,16,64,128]{0,3,2,1:T(8,128)} %copy.55, s32[240]{0:T(256)S(1)} %bitcast.72), kind=kCustom, calls=%fused_computation | custom fusion | bytes 8640 | tf_op jit(solution)/shard_map/gather | solution.py:92
  92.7 1.6 select_bitcast_fusion.1
  94.3 37.6 %psum.15 = f32[3,240]{0,1:T(8,128)} all-reduce(f32[3,240]{0,1:T(8,128)} %select_bitcast_fusion.1), channel_id=1, replica_groups=mesh['gx'=4,'gy'=8] {'gy'}, use_global_device_ids=true, to_apply=%region_1.2 | all-reduce | flops 720 | bytes 5760 | tf_op jit(solution)/shard_map/psum | solution.py:96
  136.3 1.8 fusion.39
  139.9 1.7 add_multiply_fusion
  143.2 1.4 multiply_select_fusion.1
  145.8 10.2 %while.11 = (s32[]{:T(128)}, f32[4,3,4,64,128]{4,3,2,1,0:T(8,128)}, f32[3,240]{1,0:T(4,128)S(1)}, f32[4,4,240]{2,1,0:T(4,128)}, s32[240]{0:T(256)S(1)}, /*index=5*/s32[240]{0:T(256)}, s32[128]{0:T(128)}, s32[]{:T(128)}) while((s32[]{:T(128)}, f32[4,3,4,64,128]{4,3,2,1,0:T(8,128)}, f32[3,240]{1,0:T(4,128)S(1)}, ...), condition=%wide.region_5.6_spmd.clone, body=%wide.region_4.5_spmd.clone.sunk | while | flops 48402240 | bytes 556633 | solution.py:140
  146.5 1.8 fusion.83
  149.1 1.8 fusion.83
  151.6 1.8 fusion.83
  154.2 1.8 fusion.83
  156.0 1.7 fusion.79
  158.4 4.7 %collective-permute-start.3 = (f32[3,18,64,1]{2,3,1,0:T(1,128)}, f32[3,18,64,1]{2,3,1,0:T(1,128)}, u32[]{:S(2)}, u32[]{:S(2)}) collective-permute-start(f32[3,18,64,1]{2,3,1,0:T(1,128)} %get-tuple-element.103), channel_id=1, source_target_pairs={{1,0},{2,1},{3,2},{4,3},{5,4},{6,5},{7,6},{0,7},{9,8},{10,9},{11,1... | collective-permute-start | bytes 41480 | tf_op jit(solution)/shard_map/ppermute | solution.py:36
  163.2 2.7 %copy.58 = f32[3,4,4,64,128]{4,3,2,1,0:T(8,128)} copy(f32[3,4,4,64,128]{4,3,2,0,1:T(8,128)} %bitcast.84) | data formatting | bytes 3145728 | tf_op jit(solution)/shard_map/transpose | solution.py:141
  165.9 1.6 copy.60
  168.7 1.9 slice.159
  173.9 2.6 %fusion.34 = (f32[3,16,64,128]{2,3,1,0:T(8,128)S(1)}, f32[3,16,64,128]{2,3,1,0:T(8,128)}) fusion(f32[3,1,64,130]{2,3,1,0:T(8,128)S(1)} %get-tuple-element.101, f32[3,16,64,130]{2,3,1,0:T(8,128)S(1)} %copy-done, f32[3,1,64,130]{2,3,1,0:T(8,128)S(1)} %get-tuple-element.100, f32[3,18,66,130]{2,3,1,0:T(8,128)S(1)} %select_maximum_fusion), kind=kLoop, calls=%fused_computation.58 | loop fusion | flops 2359296 | bytes 8088576 | tf_op jit(solution)/shard_map/mul | solution.py:56
  176.5 4.5 %fusion.36 = f32[3,16,64,128]{2,3,1,0:T(8,128)S(1)} fusion(f32[3,18,64,1]{2,3,1,0:T(1,128)} %collective-permute-done.3, f32[3,1,64,128]{2,3,1,0:T(8,128)S(1)} %bitcast.76, f32[3,16,64,128]{2,3,1,0:T(8,128)S(1)} %copy.42, f32[3,1,64,128]{2,3,1,0:T(8,128)S(1)} %bitcast.81, f32[3,18,64,1]{2,3,1,0:T(1,128)} %collective-permute-done.2), kind=kLoop, calls=%fused_computation.60 | loop fusion | flops 3145728 | bytes 3369984 | tf_op jit(solution)/shard_map/mul | solution.py:56
  182.9 11.7 %multiply_subtract_fusion = f32[3,16,64,128]{2,3,1,0:T(8,128)} fusion(f32[3,16,64,128]{2,3,1,0:T(8,128)S(1)} %copy.42, f32[3,18,66,130]{2,3,1,0:T(8,128)S(1)} %select_maximum_fusion, f32[3,1,64,130]{2,3,1,0:T(8,128)S(1)} %copy-done.6, f32[3,16,64,130]{2,3,1,0:T(8,128)S(1)} %copy-done, f32[3,1,64,130]{2,3,1,0:T(8,128)S(1)} %get-tuple-element.100, ...), kind=kLoop, calls=%fused_computation.55 | loop fusion | flops 11010048 | bytes 10508352 | tf_op jit(solution)/shard_map/sub | solution.py:113
  194.6 3.2 %copy.59 = f32[3,16,64,128]{3,2,1,0:T(8,128)} copy(f32[3,16,64,128]{2,3,1,0:T(8,128)} %multiply_subtract_fusion) | data formatting | bytes 3145728
  (70 shorter events, 23.5 us)
Async XLA Ops:
  7.2 163.5 %all-reduce.6.cloned.1.call-start = ((), (), s32[]{:S(2)}) async-start(), calls=%async_computation | async-start | bytes 393216 | tf_op jit(solution)/shard_map/psum | solution.py:24
  9.0 148.8 %collective-permute-start.1 = (f32[3,1,64,128]{2,3,0,1:T(8,128)}, f32[3,1,64,128]{2,3,0,1:T(8,128)S(1)}, u32[]{:S(2)}, u32[]{:S(2)}) collective-permute-start(f32[3,1,64,128]{2,3,0,1:T(8,128)} %copy.64), channel_id=1, source_target_pairs={{8,0},{16,8},{24,16},{0,24},{9,1},{17,9},{25,17},{1,25},{10,2},{18... | collective-permute-start | bytes 294920 | tf_op jit(solution)/shard_map/ppermute | solution.py:36
  53.0 104.8 %collective-permute-start = (f32[3,1,64,128]{2,3,0,1:T(8,128)}, f32[3,1,64,128]{2,3,0,1:T(8,128)S(1)}, u32[]{:S(2)}, u32[]{:S(2)}) collective-permute-start(f32[3,1,64,128]{2,3,0,1:T(8,128)} %copy.63), channel_id=1, source_target_pairs={{0,8},{8,16},{16,24},{24,0},{1,9},{9,17},{17,25},{25,1},{2,10},{10... | collective-permute-start | bytes 294920 | tf_op jit(solution)/shard_map/ppermute | solution.py:34
  55.1 33.2 %copy-start.9 = (s32[1,240]{1,0:T(1,128)S(1)}, s32[1,240]{1,0:T(1,128)}, u32[]{:S(2)}) copy-start(s32[1,240]{1,0:T(1,128)} %param.8) | copy-start | bytes 2884
  55.1 33.2 %copy-start.8 = (s32[1,3,240]{2,0,1:T(1,128)S(1)}, s32[1,3,240]{2,0,1:T(1,128)}, u32[]{:S(2)}) copy-start(s32[1,3,240]{2,0,1:T(1,128)} %param.9) | copy-start | bytes 8644
  158.4 9.0 %collective-permute-start.2 = (f32[3,18,64,1]{2,3,1,0:T(1,128)}, f32[3,18,64,1]{2,3,1,0:T(1,128)}, u32[]{:S(2)}, u32[]{:S(2)}) collective-permute-start(f32[3,18,64,1]{2,3,1,0:T(1,128)} %get-tuple-element.102), channel_id=1, source_target_pairs={{0,1},{1,2},{2,3},{3,4},{4,5},{5,6},{6,7},{7,0},{8,9},{9,10},{10,1... | collective-permute-start | bytes 41480 | tf_op jit(solution)/shard_map/ppermute | solution.py:34
  158.4 9.0 %collective-permute-start.3 = (f32[3,18,64,1]{2,3,1,0:T(1,128)}, f32[3,18,64,1]{2,3,1,0:T(1,128)}, u32[]{:S(2)}, u32[]{:S(2)}) collective-permute-start(f32[3,18,64,1]{2,3,1,0:T(1,128)} %get-tuple-element.103), channel_id=1, source_target_pairs={{1,0},{2,1},{3,2},{4,3},{5,4},{6,5},{7,6},{0,7},{9,8},{10,9},{11,1... | collective-permute-start | bytes 41480 | tf_op jit(solution)/shard_map/ppermute | solution.py:36
  170.7 2.1 %copy-start = (f32[3,16,64,130]{2,3,1,0:T(8,128)S(1)}, f32[3,16,64,130]{2,3,1,0:T(8,128)}, u32[]{:S(2)}) copy-start(f32[3,16,64,130]{2,3,1,0:T(8,128)} %slice.159) | copy-start | bytes 4792324
  172.0 1.9 copy-start.5
  176.5 4.5 %copy-start.1 = (f32[3,16,64,128]{2,3,1,0:T(8,128)S(1)}, f32[3,16,64,128]{2,3,1,0:T(8,128)}, u32[]{:S(2)}) copy-start(f32[3,16,64,128]{2,3,1,0:T(8,128)} %get-tuple-element.113) | copy-start | bytes 4718596
  181.0 1.3 copy-start.2
  181.0 1.5 copy-start.3
  181.0 1.8 copy-start.4
  181.0 1.8 copy-start.6
  181.0 1.9 copy-start.7
Sparse Core Ops, SparseCore 0:
  52.3 29.7 all-reduce.5
where the time goes:
time: 207 us; the launch traced here: 205 us
  blocking collectives  75.7 us (37%)
  local copies, waits for them, and re-layouts  60.7 us (29%)
  other arithmetic  38.8 us (19%)
  between operations  14.9 us (7%)
  matrix products  7.35 us (4%)
  starting transfers between devices  7.14 us (3%)
    unnamed x27, local copies, waits for them, and re-layouts  44.2 us
    all_gather x1, blocking collectives, local(): gathered = lax.all_gather(own_plane, 'gy', axis=2, tiled=True)  38.1 us
    psum x1, blocking collectives, local(): values = lax.psum(partial_value, 'gy')  37.6 us
    sub x1, other arithmetic, local(): tendency_core - fringe[None, :, None, None] * (center - inflow[:, None])  11.7 us
    dot_general x4, matrix products, spread_block(): jnp.dot(flattened, weight_y, preferred_element_type=jnp.float32)  7.35 us
    ppermute x2, starting transfers between devices, padded_2(): lax.ppermute(head, axis, [((i + 1) % count, i) for i in range(count)])  7.1 us
    mul x1, other arithmetic, tendency(): (y_plus - y_minus) * 0.5  4.49 us
    gather x1, local copies, waits for them, and re-layouts, local(): at_points = velocity_section[:, loc_x, levels_at, loc_y]  4.32 us
  transfers between devices with their start and end apart: 5, of which 0 were waited for; matrix products, arithmetic and copies ran while one was open for 38% of the time, Pallas kernels for 0%

commit v1 on v0

v1 whole, which is shorter than its diff:
```python
import functools
import math

import jax
import jax.numpy as jnp
from jax import lax
from jax.experimental import pallas as pl
from jax.experimental.pallas import tpu as pltpu
from jax.sharding import PartitionSpec as P

BLADES = 3
BLADE_PTS = 40


viscosity = 0.02
smag_sq = 0.0256
kernel_sq = 4.0
kernel_reach = 4
force_gain = 4.0
fringe_base = 0.05
fringe_ramp = 0.45
kernel_norm = 1.0 / math.sqrt(math.pi * kernel_sq)
TILE = 8
LANES = 128
MESH = pl.DeviceIdType.MESH


def kernel_weight(distance):
    inside = jnp.abs(distance) <= kernel_reach
    return jnp.where(inside, jnp.exp(-(distance * distance) / kernel_sq) * kernel_norm, 0.0)


def exchange(
    count_x,
    count_y,
    map_ref,
    u_ref,
    owner_ref,
    cell_ref,
    below_ref,
    above_ref,
    edge_ref,
    inflow_ref,
    values_ref,
    points,
    edges,
    got_edges,
    held,
    picked,
    parts,
    x_send,
    x_recv,
    y_send,
    y_recv,
    v_send,
    v_recv,
    p1_send,
    p1_recv,
    p2_send,
    p2_recv,
    p3_send,
    p3_recv,
):
    comps, cells_x, levels, cells_y = u_ref.shape
    pts = owner_ref.shape[1]
    padded_pts = points.shape[1]
    pieces = min(count_y, levels // TILE)
    depth = levels // pieces
    gx, gy = lax.axis_index("gx"), lax.axis_index("gy")
    source = 3 * count_x // 4
    span = [lax.rem(gy + o, count_y) for o in range(count_y)]
    stream = [lax.rem(gx + o, count_x) for o in range(count_x)]
    back = [lax.rem(gy + count_y - o, count_y) for o in range(count_y)]

    def remote(src, dst, send, recv, x=None, y=None):
        return pltpu.make_async_remote_copy(
            src_ref=src,
            dst_ref=dst,
            send_sem=send,
            recv_sem=recv,
            device_id=(gx if x is None else x, gy if y is None else y),
            device_id_type=MESH,
        )

    def rows(k):
        return pl.ds(pl.multiple_of(k * depth, depth), depth)

    barrier = pltpu.get_barrier_semaphore()
    for o in range(1, count_y):
        pl.semaphore_signal(barrier, inc=1, device_id=(gx, span[o]), device_id_type=MESH)
    for o in range(1, count_x):
        pl.semaphore_signal(barrier, inc=1, device_id=(stream[o], gy), device_id_type=MESH)
    pl.semaphore_wait(barrier, count_y + count_x - 2)

    def first(o):
        return remote(
            u_ref.at[:, 0, rows(span[o])], held.at[gy], p1_send.at[o], p1_recv.at[gy], y=span[o]
        )

    @pl.when(gx == source)
    def _():
        for o in range(1, count_y):
            if pieces == count_y:
                first(o).start()
            else:
                pl.when(span[o] < pieces)(lambda o=o: first(o).start())

    up = remote(u_ref.at[:, cells_x - 1], below_ref, x_send.at[0], x_recv.at[0], x=stream[1])
    down = remote(
        u_ref.at[:, 0], above_ref, x_send.at[1], x_recv.at[1], x=stream[count_x - 1]
    )
    pl.when(gx < count_x - 1)(lambda: up.start())
    pl.when(gx > 0)(lambda: down.start())

    lane = lax.broadcasted_iota(jnp.int32, (levels, LANES), 1)
    packed = jnp.zeros((levels, LANES), jnp.float32)
    slot = lax.div(lax.rem(lane + 1, LANES), 2)
    for c in range(comps):
        for x in range(cells_x):
            n = c * cells_x + x
            packed = jnp.where(slot == n, pltpu.roll(u_ref[c, x], 2 * n, 1), packed)
    edges[...] = packed
    right = remote(edges, got_edges.at[0], y_send.at[0], y_recv.at[0], y=span[1])
    left = remote(edges, got_edges.at[1], y_send.at[1], y_recv.at[1], y=span[count_y - 1])
    right.start()
    left.start()

    def second(o):
        return remote(
            picked.at[span[o]],
            inflow_ref.at[:, rows(gy)],
            p2_send.at[o],
            p2_recv.at[gy],
            y=span[o],
        )

    def second_leg():
        held[gy] = u_ref[:, 0, rows(gy), :]
        for o in range(1, count_y):
            remote(
                held.at[back[o]], held.at[back[o]], p1_send.at[o], p1_recv.at[back[o]], y=back[o]
            ).wait_recv()
        for j in range(count_y):
            picked[j] = held[map_ref[j]]
        for o in range(1, count_y):
            second(o).start()
        inflow_ref[:, rows(gy), :] = picked[gy]

    @pl.when(gx == source)
    def _():
        if pieces == count_y:
            second_leg()
        else:
            pl.when(gy < pieces)(second_leg)

    points[...] = jnp.zeros_like(points)
    points[2:3, :] = jnp.full((1, padded_pts), -1, jnp.int32)
    points[0:1, 0:pts] = cell_ref[0, 0:1, :] * levels + cell_ref[0, 2:3, :]
    points[1:2, 0:pts] = cell_ref[0, 1:2, :]
    points[2:3, 0:pts] = owner_ref[...]

    def down_rows(row):
        spread = jnp.broadcast_to(row.astype(jnp.float32), (LANES, padded_pts))
        return spread.T

    flat = down_rows(points[0:1, :])
    at_y = down_rows(points[1:2, :])
    own = down_rows(points[2:3, :])
    lanes = lax.broadcasted_iota(jnp.int32, (padded_pts, LANES), 1).astype(jnp.float32)
    mine = (at_y == lanes) & (own == gy.astype(jnp.float32))
    chosen = jnp.concatenate(
        [
            jnp.where(flat == lanes + float(t * LANES), 1.0, 0.0).astype(jnp.bfloat16)
            for t in range(cells_x * levels // LANES)
        ],
        axis=1,
    )
    at_points = jnp.zeros((padded_pts, LANES), jnp.float32)
    for c in range(comps):
        field = u_ref[c].reshape(cells_x * levels, cells_y)
        total = jnp.zeros((padded_pts, LANES), jnp.float32)
        for _ in range(3):
            part = field.astype(jnp.bfloat16)
            total = total + jnp.dot(chosen, part, preferred_element_type=jnp.float32)
            field = field - part.astype(jnp.float32)
        column = jnp.sum(jnp.where(mine, total, 0.0), axis=1, keepdims=True)
        at_points = jnp.where(lanes == float(c), column, at_points)
    parts[gy] = at_points.T[0:TILE]

    def share(o):
        return remote(parts.at[gy], parts.at[gy], v_send.at[o], v_recv.at[gy], y=span[o])

    for o in range(1, count_y):
        share(o).start()

    def third(o, k):
        return remote(
            inflow_ref.at[:, rows(k)],
            inflow_ref.at[:, rows(k)],
            p3_send.at[o, k],
            p3_recv.at[k],
            x=stream[o],
        )

    def forward(q):
        k = lax.rem(gy + count_y - q, count_y)

        def arrived():
            remote(
                picked.at[0], inflow_ref.at[:, rows(k)], p2_send.at[0], p2_recv.at[k], y=back[1]
            ).wait_recv()

        def send_on():
            if q > 0:
                arrived()
            for o in range(1, count_x):
                third(o, k).start()

        if pieces == count_y:
            send_on()
        else:
            pl.when(k < pieces)(send_on)

    @pl.when(gx == source)
    def _():
        for q in range(count_y):
            forward(q)

    for side in range(2):
        remote(edges, got_edges.at[side], y_send.at[side], y_recv.at[side], y=span[1]).wait_recv()
    even = lax.rem(lane, 2) == 0
    edge_ref[...] = jnp.where(
        even, pltpu.roll(got_edges[0], 1, 1), pltpu.roll(got_edges[1], LANES - 1, 1)
    )

    for o in range(1, count_y):
        remote(
            parts.at[back[o]], parts.at[back[o]], v_send.at[o], v_recv.at[back[o]], y=back[o]
        ).wait_recv()
    values = parts[0]
    for j in range(1, count_y):
        values = values + parts[j]
    values_ref[...] = values

    pl.when(gx > 0)(lambda: up.wait_recv())
    pl.when(gx < count_x - 1)(lambda: down.wait_recv())

    @pl.when(gx == count_x - 1)
    def _():
        above_ref[...] = u_ref[:, cells_x - 1]

    @pl.when(gx != source)
    def _():
        for k in range(pieces):
            third(1, k).wait_recv()

    @pl.when(gx == 0)
    def _():
        below_ref[...] = inflow_ref[...]

    pl.when(gx < count_x - 1)(lambda: up.wait_send())
    pl.when(gx > 0)(lambda: down.wait_send())
    right.wait_send()
    left.wait_send()
    for o in range(1, count_y):
        share(o).wait_send()

    @pl.when(gx == source)
    def _():
        for o in range(1, count_y):
            if pieces == count_y:
                first(o).wait_send()
                second(o).wait_send()
            else:
                pl.when(span[o] < pieces)(lambda o=o: first(o).wait_send())
                pl.when(gy < pieces)(lambda o=o: second(o).wait_send())
        for o in range(1, count_x):
            for k in range(pieces):
                third(o, k).wait_send()


def compute(
    count_x,
    count_y,
    u_ref,
    below_ref,
    above_ref,
    edge_ref,
    inflow_ref,
    values_ref,
    owner_ref,
    cell_ref,
    gain_ref,
    rate_ref,
    spread_ref,
    force_ref,
    points,
    gains,
    cells,
    rate,
    spread,
    in_sem,
    rate_sem,
    spread_sem,
):
    comps, cells_x, levels, cells_y = rate.shape
    pts = owner_ref.shape[1]
    padded_pts = points.shape[1]
    per_turb = BLADES * BLADE_PTS
    gx, gy = lax.axis_index("gx"), lax.axis_index("gy")

    fetch = pltpu.make_async_copy(u_ref, cells.at[:, pl.ds(1, cells_x)], in_sem)
    fetch.start()
    cells[:, 0] = below_ref[...]
    cells[:, cells_x + 1] = above_ref[...]

    points[...] = jnp.zeros_like(points)
    gains[...] = jnp.zeros_like(gains)
    points[0:1, 0:pts] = cell_ref[0, 0:1, :]
    points[1:2, 0:pts] = owner_ref[...] * cells_y + cell_ref[0, 1:2, :]
    points[2:3, 0:pts] = cell_ref[0, 2:3, :]
    gains[0:1, 0:pts] = gain_ref[...]
    gain = gains[0:1, :]
    at = [values_ref[c : c + 1, :] for c in range(comps)]
    row = lax.broadcasted_iota(jnp.int32, (1, padded_pts), 1)
    axial = jnp.zeros((1, padded_pts), jnp.float32)
    for t in range(pts // per_turb):
        inside = (row >= t * per_turb) & (row < (t + 1) * per_turb)
        mean = jnp.sum(jnp.where(inside, at[0], 0.0), axis=1, keepdims=True) * (1.0 / per_turb)
        axial = jnp.where(inside, mean * mean, axial)
    speed = jnp.sqrt(at[0] * at[0] + at[1] * at[1] + at[2] * at[2])
    forces = []
    for c in range(comps):
        drive = speed * at[c]
        if c == 0:
            drive = drive + axial
        forces.append(-force_gain * gain * drive)
        force_ref[0, c : c + 1, :] = forces[c][:, 0:pts]

    level = lax.broadcasted_iota(jnp.int32, (levels, padded_pts), 0)
    weight_z = kernel_weight((level - points[2:3, :]).astype(jnp.float32))
    span_total = count_y * cells_y
    y_cell = lax.broadcasted_iota(jnp.int32, (cells_y, padded_pts), 0) + gy * cells_y
    distance = y_cell - points[1:2, :]
    distance = jnp.where(distance >= span_total // 2, distance - span_total, distance)
    distance = jnp.where(distance < -(span_total // 2), distance + span_total, distance)
    weight_y = kernel_weight(distance.astype(jnp.float32)).astype(jnp.bfloat16)
    point_x = points[0:1, :]

    lane = lax.broadcasted_iota(jnp.int32, (levels, cells_y), 1)
    deep = lax.broadcasted_iota(jnp.int32, (levels, cells_y), 0)
    fetch.wait()

    def plane(x):
        weight_x = kernel_weight((x - point_x).astype(jnp.float32))
        weighted = jnp.concatenate(
            [((forces[c] * weight_x) * weight_z).astype(jnp.bfloat16) for c in range(comps)], 0
        )
        spread[:, x] = lax.dot_general(
            weighted, weight_y, (((1,), (1,)), ((), ())), preferred_element_type=jnp.float32
        ).reshape(comps, levels, cells_y)
        pltpu.make_async_copy(spread.at[:, x], spread_ref.at[:, x], spread_sem.at[x]).start()

        center, grads, sums = [], [[], [], []], []
        for c in range(comps):
            here, plus, minus = cells[c, x + 1], cells[c, x + 2], cells[c, x]
            n = 2 * (c * cells_x + x)
            side = pltpu.roll(edge_ref[...], lax.rem(LANES - n, LANES), 1)
            y_minus = jnp.where(lane == 0, side, pltpu.roll(here, 1, 1))
            y_plus = jnp.where(lane == cells_y - 1, side, pltpu.roll(here, cells_y - 1, 1))
            z_minus = jnp.where(deep == 0, 0.0, pltpu.roll(here, 1, 0))
            z_plus = jnp.where(deep == levels - 1, 0.0, pltpu.roll(here, levels - 1, 0))
            center.append(here)
            grads[0].append((plus - minus) * 0.5)
            grads[1].append((y_plus - y_minus) * 0.5)
            grads[2].append((z_plus - z_minus) * 0.5)
            sums.append(plus + minus + y_plus + y_minus + z_plus + z_minus - 6.0 * here)
        diagonal = grads[0][0] * grads[0][0] + grads[1][1] * grads[1][1] + grads[2][2] * grads[2][2]
        s01 = grads[0][1] + grads[1][0]
        s02 = grads[0][2] + grads[2][0]
        s12 = grads[1][2] + grads[2][1]
        twice = 2.0 * diagonal + (s01 * s01 + s02 * s02 + s12 * s12)
        eddy = viscosity + smag_sq * jnp.sqrt(twice)
        x_glob = (gx * cells_x + x).astype(jnp.float32)
        fringe = fringe_base + fringe_ramp * (x_glob + 0.5) * (1.0 / (count_x * cells_x))
        for c in range(comps):
            advect = center[0] * grads[0][c] + center[1] * grads[1][c] + center[2] * grads[2][c]
            rate[c, x] = eddy * sums[c] - advect - fringe * (center[c] - inflow_ref[c])
        pltpu.make_async_copy(rate.at[:, x], rate_ref.at[:, x], rate_sem.at[x]).start()

    lax.fori_loop(0, cells_x, lambda x, carry: (plane(x), carry)[1], 0)

    def finish(x):
        pltpu.make_async_copy(spread.at[:, x], spread_ref.at[:, x], spread_sem.at[x]).wait()
        pltpu.make_async_copy(rate.at[:, x], rate_ref.at[:, x], rate_sem.at[x]).wait()

    lax.fori_loop(0, cells_x, lambda x, carry: (finish(x), carry)[1], 0)


def local(velocity_section, point_owner, point_cell, blade_coef, recycle_map):
    comps, cells_x, levels, cells_y = velocity_section.shape
    pts = point_owner.shape[1]
    padded_pts = -(-pts // LANES) * LANES
    count_x, count_y = lax.axis_size("gx"), lax.axis_size("gy")
    pieces = min(count_y, levels // TILE)
    depth = levels // pieces
    vmem = pl.BlockSpec(memory_space=pltpu.VMEM)
    smem = pl.BlockSpec(memory_space=pltpu.SMEM)
    hbm = pl.BlockSpec(memory_space=pl.ANY)
    f32 = jnp.float32
    plane = jax.ShapeDtypeStruct((comps, levels, cells_y), f32)
    dma = pltpu.SemaphoreType.DMA
    below, above, edge, inflow, values = pl.pallas_call(
        functools.partial(exchange, count_x, count_y),
        out_shape=(
            plane,
            plane,
            jax.ShapeDtypeStruct((levels, LANES), f32),
            plane,
            jax.ShapeDtypeStruct((TILE, padded_pts), f32),
        ),
        in_specs=[smem, vmem, vmem, vmem],
        out_specs=(vmem,) * 5,
        scratch_shapes=[
            pltpu.VMEM((TILE, padded_pts), jnp.int32),
            pltpu.VMEM((levels, LANES), f32),
            pltpu.VMEM((2, levels, LANES), f32),
            pltpu.VMEM((count_y, comps, depth, cells_y), f32),
            pltpu.VMEM((count_y, comps, depth, cells_y), f32),
            pltpu.VMEM((count_y, TILE, padded_pts), f32),
            dma((2,)),
            dma((2,)),
            dma((2,)),
            dma((2,)),
            dma((count_y,)),
            dma((count_y,)),
            dma((count_y,)),
            dma((count_y,)),
            dma((count_y,)),
            dma((count_y,)),
            dma((count_x, pieces)),
            dma((pieces,)),
        ],
        compiler_params=pltpu.CompilerParams(
            collective_id=0, has_side_effects=True, vmem_limit_bytes=32 * 1024 * 1024
        ),
        name="exchange",
    )(recycle_map, velocity_section, point_owner, point_cell)
    return pl.pallas_call(
        functools.partial(compute, count_x, count_y),
        out_shape=(
            jax.ShapeDtypeStruct(velocity_section.shape, f32),
            jax.ShapeDtypeStruct(velocity_section.shape, f32),
            jax.ShapeDtypeStruct((1, comps, pts), f32),
        ),
        in_specs=[hbm] + [vmem] * 8,
        out_specs=(hbm, hbm, vmem),
        scratch_shapes=[
            pltpu.VMEM((TILE, padded_pts), jnp.int32),
            pltpu.VMEM((TILE, padded_pts), f32),
            pltpu.VMEM((comps, cells_x + 2, levels, cells_y), f32),
            pltpu.VMEM(velocity_section.shape, f32),
            pltpu.VMEM(velocity_section.shape, f32),
            dma(()),
            dma((cells_x,)),
            dma((cells_x,)),
        ],
        compiler_params=pltpu.CompilerParams(vmem_limit_bytes=32 * 1024 * 1024),
        name="compute",
    )(
        velocity_section,
        below,
        above,
        edge,
        inflow,
        values,
        point_owner,
        point_cell,
        blade_coef,
    )


def solution(mesh):
    placed = (P(None, "gx", None, "gy"), P("gx", None), P("gx", None, None), P("gx", None), P())
    return jax.shard_map(
        local,
        mesh=mesh,
        in_specs=placed,
        out_specs=(P(None, "gx", None, "gy"), P(None, "gx", None, "gy"), P("gx", None, None)),
        check_vma=False,
    )
```

time: 207 us -> 28 us (0.14); the launches traced: 205 us -> 27.8 us
  blocking collectives: 75.7 us -> 0 us
  local copies, waits for them, and re-layouts: 60.7 us -> 4.02 us
  other arithmetic: 38.8 us -> 0 us
  Pallas kernels: 0 us -> 23.1 us
  between operations: 14.9 us -> 0.67 us
  matrix products: 7.35 us -> 0 us
  starting transfers between devices: 7.14 us -> 0 us
    unnamed x27 -> x11, local copies, waits for them, and re-layouts: 44.2 us -> 3.44 us
    all_gather x1 -> x0, blocking collectives: 38.1 us -> none  [local(): gathered = lax.all_gather(own_plane, 'gy', axis=2, tiled=True)]
    psum x1 -> x0, blocking collectives: 37.6 us -> none  [local(): values = lax.psum(partial_value, 'gy')]
    pallas_call x0 -> x2, Pallas kernels: none -> 23.1 us  [the longest x1 18.1 us: local(): pl.pallas_call(functools.partial(exchange, count_x, count_y), out_shape=(...]
    mul x12 -> x0, other arithmetic: 13.8 us -> none  [the longest x1 4.49 us: tendency(): (y_plus - y_minus) * 0.5]
    sub x2 -> x0, other arithmetic: 12.2 us -> none  [the longest x1 11.7 us: local(): tendency_core - fringe[None, :, None, None] * (center - inflow[:, None])]
    dot_general x4 -> x0, matrix products: 7.35 us -> none  [spread_block(): jnp.dot(flattened, weight_y, preferred_element_type=jnp.float32)]
    ppermute x4 -> x0, starting transfers between devices: 7.1 us -> none  [the longest x2 7.1 us: padded_2(): lax.ppermute(head, axis, [((i + 1) % count, i) for i in range(count)])]
  transfers between devices with their start and end apart: 5 -> 0, of which waited for: 0 -> 0; matrix products, arithmetic and copies ran while one was open for 38% -> 0% of each run, Pallas kernels for 0% -> 0%
where the time goes in v1:
time: 28 us; the launch traced here: 27.8 us
  Pallas kernels  23.1 us (82%)
  local copies, waits for them, and re-layouts  4.02 us (14%)
  between operations  0.67 us (2%)
    pallas_call x1, Pallas kernels, local(): pl.pallas_call(functools.partial(exchange, count_x, count_y), out_shape=(...  18.1 us
    pallas_call x1, Pallas kernels, local(): pl.pallas_call(functools.partial(compute, count_x, count_y), out_shape=(j...  5 us
    unnamed x11, local copies, waits for them, and re-layouts  3.44 us
    pallas_call x1, local copies, waits for them, and re-layouts, local(): pl.pallas_call(functools.partial(compute, count_x, count_y), out_shape=(j...  0.58 us

profile of v1, /device:TPU:0, one launch (start us, length us, event | category | flops | bytes accessed | tf_op | source)
XLA Modules:
  0.0 27.8 jit_solution(3029597099253311938)
XLA Ops:
  0.6 0.0 copy-start.3
  0.6 0.7 %copy.8.cell_ref = s32[1,3,240]{2,1,0:T(4,128)S(1)} copy(s32[1,3,240]{2,0,1:T(1,128)} %param.7) | data formatting | bytes 5760 | tf_op args[2]
  1.3 0.0 copy-start
  1.3 1.4 %copy-done = f32[3,16,64,128]{3,2,1,0:T(8,128)S(1)} copy-done((f32[3,16,64,128]{3,2,1,0:T(8,128)S(1)}, f32[3,16,64,128]{3,2,1,0:T(8,128)}, u32[]{:S(2)}) %copy-start) | copy-done | bytes 1572888
  2.7 0.0 copy-start.2
  2.7 0.7 %copy-done.2 = s32[1,240]{1,0:T(1,128)S(1)} copy-done((s32[1,240]{1,0:T(1,128)S(1)}, s32[1,240]{1,0:T(1,128)}, u32[]{:S(2)}) %copy-start.2) | copy-done | bytes 984
  3.4 0.0 copy-start.4
  3.4 0.7 %copy-done.4 = s32[8]{0:T(128)S(1)} copy-done((s32[8]{0:T(128)S(1)}, s32[8]{0:T(128)}, u32[]{:S(2)}) %copy-start.4) | copy-done | bytes 56
  4.1 0.0 copy-start.1
  4.1 18.1 %exchange.1 = (f32[3,64,128]{2,1,0:T(8,128)S(1)}, f32[3,64,128]{2,1,0:T(8,128)S(1)}, f32[64,128]{1,0:T(8,128)S(1)}, f32[3,64,128]{2,1,0:T(8,128)S(1)}, f32[8,256]{1,0:T(8,128)S(1)}) custom-call(s32[8]{0:T(128)S(1)} %copy-done.4, f32[3,16,64,128]{3,2,1,0:T(8,128)S(1)} %copy-done, s32[1,240]{1,0:T(1,128)S(1)} %copy-done.2, s32[1,3,240]{2,1,0:T(4,128)S(1)} %copy.8.cell_ref), custom_call_target="tpu_custom_call" | custom-call | tf_op jit(solution)/shard_map/exchange/pallas_call | solution.py:413
  22.2 0.0 copy-done.3
  22.2 0.0 copy-done.1
  22.2 5.0 %compute.1 = (f32[3,16,64,128]{3,2,1,0:T(8,128)}, f32[3,16,64,128]{3,2,1,0:T(8,128)}, f32[1,3,240]{2,1,0:T(4,128)S(1)}) custom-call(f32[3,16,64,128]{3,2,1,0:T(8,128)S(1)} %copy-done.1, f32[3,64,128]{2,1,0:T(8,128)S(1)} %get-tuple-element.8.below_ref, f32[3,64,128]{2,1,0:T(8,128)S(1)} %get-tuple-element.9.above_ref, ...), custom_call_target="tpu_custom_call" | custom-call | tf_op jit(solution)/shard_map/compute/pallas_call | solution.py:449
  27.2 0.6 %copy.10 = f32[1,3,240]{2,0,1:T(1,128)} copy(f32[1,3,240]{2,1,0:T(4,128)S(1)} %get-tuple-element.15) | data formatting | bytes 5760 | tf_op jit(solution)/shard_map/compute/pallas_call | solution.py:449
Async XLA Ops:
  0.6 21.6 %copy-start.3 = (f32[1,240]{1,0:T(1,128)S(1)}, f32[1,240]{1,0:T(1,128)}, u32[]{:S(2)}) copy-start(f32[1,240]{1,0:T(1,128)} %gain_ref.1) | copy-start | bytes 2884
  1.3 1.4 %copy-start = (f32[3,16,64,128]{3,2,1,0:T(8,128)S(1)}, f32[3,16,64,128]{3,2,1,0:T(8,128)}, u32[]{:S(2)}) copy-start(f32[3,16,64,128]{3,2,1,0:T(8,128)} %u_ref.3) | copy-start | bytes 4718596
  2.7 0.7 %copy-start.2 = (s32[1,240]{1,0:T(1,128)S(1)}, s32[1,240]{1,0:T(1,128)}, u32[]{:S(2)}) copy-start(s32[1,240]{1,0:T(1,128)} %owner_ref.3) | copy-start | bytes 2884
  3.4 0.7 %copy-start.4 = (s32[8]{0:T(128)S(1)}, s32[8]{0:T(128)}, u32[]{:S(2)}) copy-start(s32[8]{0:T(128)} %map_ref.1) | copy-start | bytes 100
  4.1 18.1 %copy-start.1 = (f32[3,16,64,128]{3,2,1,0:T(8,128)S(1)}, f32[3,16,64,128]{3,2,1,0:T(8,128)}, u32[]{:S(2)}) copy-start(f32[3,16,64,128]{3,2,1,0:T(8,128)} %u_ref.3) | copy-start | bytes 4718596

commit v2 on v1

v2 whole, which is shorter than its diff:
```python
import functools
import math

import jax
import jax.numpy as jnp
from jax import lax
from jax.experimental import pallas as pl
from jax.experimental.pallas import tpu as pltpu
from jax.sharding import PartitionSpec as P

BLADES = 3
BLADE_PTS = 40


viscosity = 0.02
smag_sq = 0.0256
kernel_sq = 4.0
kernel_reach = 4
force_gain = 4.0
fringe_base = 0.05
fringe_ramp = 0.45
kernel_norm = 1.0 / math.sqrt(math.pi * kernel_sq)
TILE = 8
LANES = 128
MESH = pl.DeviceIdType.MESH


def kernel_weight(distance):
    inside = jnp.abs(distance) <= kernel_reach
    return jnp.where(inside, jnp.exp(-(distance * distance) / kernel_sq) * kernel_norm, 0.0)


def evolve(
    count_x,
    count_y,
    u_ref,
    owner_ref,
    cell_ref,
    gain_ref,
    map_ref,
    core_ref,
    spread_ref,
    inflow_ref,
    force_ref,
    cells,
    owner_in,
    cell_in,
    gain_in,
    order,
    points,
    gains,
    edges,
    got_edges,
    held,
    picked,
    parts,
    in_sem,
    x_send,
    x_recv,
    y_send,
    y_recv,
    v_send,
    v_recv,
    p1_send,
    p1_recv,
    p2_send,
    p2_recv,
    p3_send,
    p3_recv,
):
    comps, cells_x, levels, cells_y = u_ref.shape
    pts = owner_ref.shape[1]
    padded_pts = points.shape[1]
    pieces = min(count_y, levels // TILE)
    depth = levels // pieces
    per_turb = BLADES * BLADE_PTS
    gx, gy = lax.axis_index("gx"), lax.axis_index("gy")
    source = 3 * count_x // 4
    span = [lax.rem(gy + o, count_y) for o in range(count_y)]
    stream = [lax.rem(gx + o, count_x) for o in range(count_x)]
    back = [lax.rem(gy + count_y - o, count_y) for o in range(count_y)]

    def remote(src, dst, send, recv, x=None, y=None):
        return pltpu.make_async_remote_copy(
            src_ref=src,
            dst_ref=dst,
            send_sem=send,
            recv_sem=recv,
            device_id=(gx if x is None else x, gy if y is None else y),
            device_id_type=MESH,
        )

    def rows(k):
        return pl.ds(pl.multiple_of(k * depth, depth), depth)

    barrier = pltpu.get_barrier_semaphore()
    for o in range(1, count_y):
        pl.semaphore_signal(barrier, inc=1, device_id=(gx, span[o]), device_id_type=MESH)
    for o in range(1, count_x):
        pl.semaphore_signal(barrier, inc=1, device_id=(stream[o], gy), device_id_type=MESH)
    fetches = [
        pltpu.make_async_copy(src, dst, in_sem.at[n])
        for n, (src, dst) in enumerate(
            [
                (u_ref, cells.at[:, pl.ds(1, cells_x)]),
                (owner_ref, owner_in),
                (cell_ref, cell_in),
                (gain_ref, gain_in),
                (map_ref, order),
            ]
        )
    ]
    for fetch in fetches:
        fetch.start()
    pl.semaphore_wait(barrier, count_y + count_x - 2)

    def first(o):
        return remote(
            u_ref.at[:, 0, rows(span[o])], held.at[gy], p1_send.at[o], p1_recv.at[gy], y=span[o]
        )

    @pl.when(gx == source)
    def _():
        for o in range(1, count_y):
            if pieces == count_y:
                first(o).start()
            else:
                pl.when(span[o] < pieces)(lambda o=o: first(o).start())

    up = remote(
        u_ref.at[:, cells_x - 1], cells.at[:, 0], x_send.at[0], x_recv.at[0], x=stream[1]
    )
    down = remote(
        u_ref.at[:, 0],
        cells.at[:, cells_x + 1],
        x_send.at[1],
        x_recv.at[1],
        x=stream[count_x - 1],
    )
    pl.when(gx < count_x - 1)(lambda: up.start())
    pl.when(gx > 0)(lambda: down.start())

    for fetch in fetches:
        fetch.wait()

    @pl.when(gx == count_x - 1)
    def _():
        cells[:, cells_x + 1] = cells[:, cells_x]

    lane = lax.broadcasted_iota(jnp.int32, (levels, LANES), 1)
    packed = jnp.zeros((levels, LANES), jnp.float32)
    slot = lax.div(lax.rem(lane + 1, LANES), 2)
    for c in range(comps):
        for x in range(cells_x):
            n = c * cells_x + x
            packed = jnp.where(slot == n, pltpu.roll(cells[c, x + 1], 2 * n, 1), packed)
    edges[...] = packed
    right = remote(edges, got_edges.at[0], y_send.at[0], y_recv.at[0], y=span[1])
    left = remote(edges, got_edges.at[1], y_send.at[1], y_recv.at[1], y=span[count_y - 1])
    right.start()
    left.start()

    def second(o):
        return remote(
            picked.at[span[o]],
            inflow_ref.at[:, rows(gy)],
            p2_send.at[o],
            p2_recv.at[gy],
            y=span[o],
        )

    def second_leg():
        held[gy] = cells[:, 1, rows(gy), :]
        for o in range(1, count_y):
            remote(
                held.at[back[o]], held.at[back[o]], p1_send.at[o], p1_recv.at[back[o]], y=back[o]
            ).wait_recv()
        for j in range(count_y):
            picked[j] = held[order[j]]
        for o in range(1, count_y):
            second(o).start()
        inflow_ref[:, rows(gy), :] = picked[gy]

    @pl.when(gx == source)
    def _():
        if pieces == count_y:
            second_leg()
        else:
            pl.when(gy < pieces)(second_leg)

    points[...] = jnp.zeros_like(points)
    gains[...] = jnp.zeros_like(gains)
    points[0:1, 0:pts] = cell_in[0] * levels + cell_in[2]
    points[1:2, 0:pts] = cell_in[1]
    points[2:3, :] = jnp.full((1, padded_pts), -1, jnp.int32)
    points[2:3, 0:pts] = owner_in[...]
    points[3:4, 0:pts] = cell_in[0]
    points[4:5, 0:pts] = owner_in[...] * cells_y + cell_in[1]
    points[5:6, 0:pts] = cell_in[2]
    gains[0:1, 0:pts] = gain_in[...]

    def down_rows(row):
        wide = jnp.broadcast_to(row.astype(jnp.float32), (LANES, padded_pts))
        return wide.T

    flat = down_rows(points[0:1, :])
    at_y = down_rows(points[1:2, :])
    own = down_rows(points[2:3, :])
    lanes = lax.broadcasted_iota(jnp.int32, (padded_pts, LANES), 1).astype(jnp.float32)
    mine = (at_y == lanes) & (own == gy.astype(jnp.float32))
    chosen = jnp.concatenate(
        [
            jnp.where(flat == lanes + float(t * LANES), 1.0, 0.0).astype(jnp.bfloat16)
            for t in range(cells_x * levels // LANES)
        ],
        axis=1,
    )
    at_points = jnp.zeros((padded_pts, LANES), jnp.float32)
    for c in range(comps):
        field = cells[c, 1 : cells_x + 1].reshape(cells_x * levels, cells_y)
        total = jnp.zeros((padded_pts, LANES), jnp.float32)
        for _ in range(3):
            part = field.astype(jnp.bfloat16)
            total = total + jnp.dot(chosen, part, preferred_element_type=jnp.float32)
            field = field - part.astype(jnp.float32)
        column = jnp.sum(jnp.where(mine, total, 0.0), axis=1, keepdims=True)
        at_points = jnp.where(lanes == float(c), column, at_points)
    parts[gy] = at_points.T[0:TILE]

    def share(o):
        return remote(parts.at[gy], parts.at[gy], v_send.at[o], v_recv.at[gy], y=span[o])

    for o in range(1, count_y):
        share(o).start()

    def third(o, k):
        return remote(
            inflow_ref.at[:, rows(k)],
            inflow_ref.at[:, rows(k)],
            p3_send.at[o, k],
            p3_recv.at[k],
            x=stream[o],
        )

    def forward(q):
        k = lax.rem(gy + count_y - q, count_y)

        def arrived():
            remote(
                picked.at[0], inflow_ref.at[:, rows(k)], p2_send.at[0], p2_recv.at[k], y=back[1]
            ).wait_recv()

        def send_on():
            if q > 0:
                arrived()
            for o in range(1, count_x):
                third(o, k).start()

        if pieces == count_y:
            send_on()
        else:
            pl.when(k < pieces)(send_on)

    @pl.when(gx == source)
    def _():
        for q in range(count_y):
            forward(q)

    for side in range(2):
        remote(edges, got_edges.at[side], y_send.at[side], y_recv.at[side], y=span[1]).wait_recv()
    right.wait_send()
    left.wait_send()
    even = lax.rem(lane, 2) == 0
    edges[...] = jnp.where(
        even, pltpu.roll(got_edges[0], 1, 1), pltpu.roll(got_edges[1], LANES - 1, 1)
    )

    deep = lax.broadcasted_iota(jnp.int32, (levels, cells_y), 0)

    def tendency(x):
        center, grads, sums = [], [[], [], []], []
        for c in range(comps):
            here, plus, minus = cells[c, x + 1], cells[c, x + 2], cells[c, x]
            n = 2 * (c * cells_x + x)
            side = pltpu.roll(edges[...], lax.rem(LANES - n, LANES), 1)
            y_minus = jnp.where(lane == 0, side, pltpu.roll(here, 1, 1))
            y_plus = jnp.where(lane == cells_y - 1, side, pltpu.roll(here, cells_y - 1, 1))
            z_minus = jnp.where(deep == 0, 0.0, pltpu.roll(here, 1, 0))
            z_plus = jnp.where(deep == levels - 1, 0.0, pltpu.roll(here, levels - 1, 0))
            center.append(here)
            grads[0].append((plus - minus) * 0.5)
            grads[1].append((y_plus - y_minus) * 0.5)
            grads[2].append((z_plus - z_minus) * 0.5)
            sums.append(plus + minus + y_plus + y_minus + z_plus + z_minus - 6.0 * here)
        diagonal = grads[0][0] * grads[0][0] + grads[1][1] * grads[1][1] + grads[2][2] * grads[2][2]
        s01 = grads[0][1] + grads[1][0]
        s02 = grads[0][2] + grads[2][0]
        s12 = grads[1][2] + grads[2][1]
        twice = 2.0 * diagonal + (s01 * s01 + s02 * s02 + s12 * s12)
        eddy = viscosity + smag_sq * jnp.sqrt(twice)
        fringe = fringe_at(gx, x, count_x, cells_x)
        for c in range(comps):
            advect = center[0] * grads[0][c] + center[1] * grads[1][c] + center[2] * grads[2][c]
            core_ref[c, x] = eddy * sums[c] - advect - fringe * center[c]

    def planes(low, high):
        lax.fori_loop(low, high, lambda x, carry: (tendency(x), carry)[1], 0)

    planes(1, cells_x - 1)

    for o in range(1, count_y):
        remote(
            parts.at[back[o]], parts.at[back[o]], v_send.at[o], v_recv.at[back[o]], y=back[o]
        ).wait_recv()
    values = parts[0]
    for j in range(1, count_y):
        values = values + parts[j]
    gain = gains[0:1, :]
    at = [values[c : c + 1] for c in range(comps)]
    row = lax.broadcasted_iota(jnp.int32, (1, padded_pts), 1)
    axial = jnp.zeros((1, padded_pts), jnp.float32)
    for t in range(pts // per_turb):
        inside = (row >= t * per_turb) & (row < (t + 1) * per_turb)
        mean = jnp.sum(jnp.where(inside, at[0], 0.0), axis=1, keepdims=True) * (1.0 / per_turb)
        axial = jnp.where(inside, mean * mean, axial)
    speed = jnp.sqrt(at[0] * at[0] + at[1] * at[1] + at[2] * at[2])
    forces = []
    for c in range(comps):
        drive = speed * at[c]
        if c == 0:
            drive = drive + axial
        forces.append(-force_gain * gain * drive)
        force_ref[c] = forces[c][:, 0:pts]

    level = lax.broadcasted_iota(jnp.int32, (levels, padded_pts), 0)
    weight_z = kernel_weight((level - points[5:6, :]).astype(jnp.float32))
    span_total = count_y * cells_y
    y_cell = lax.broadcasted_iota(jnp.int32, (cells_y, padded_pts), 0) + gy * cells_y
    distance = y_cell - points[4:5, :]
    distance = jnp.where(distance >= span_total // 2, distance - span_total, distance)
    distance = jnp.where(distance < -(span_total // 2), distance + span_total, distance)
    weight_y = kernel_weight(distance.astype(jnp.float32)).astype(jnp.bfloat16)
    point_x = points[3:4, :]

    def spread(x):
        weight_x = kernel_weight((x - point_x).astype(jnp.float32))
        weighted = jnp.concatenate(
            [((forces[c] * weight_x) * weight_z).astype(jnp.bfloat16) for c in range(comps)], 0
        )
        spread_ref[:, x] = lax.dot_general(
            weighted, weight_y, (((1,), (1,)), ((), ())), preferred_element_type=jnp.float32
        ).reshape(comps, levels, cells_y)

    lax.fori_loop(0, cells_x, lambda x, carry: (spread(x), carry)[1], 0)

    pl.when(gx > 0)(lambda: up.wait_recv())
    pl.when(gx < count_x - 1)(lambda: down.wait_recv())
    planes(cells_x - 1, cells_x)

    @pl.when(gx != source)
    def _():
        for k in range(pieces):
            third(1, k).wait_recv()

    @pl.when(gx == 0)
    def _():
        cells[:, 0] = inflow_ref[...]

    planes(0, 1)

    pl.when(gx < count_x - 1)(lambda: up.wait_send())
    pl.when(gx > 0)(lambda: down.wait_send())
    for o in range(1, count_y):
        share(o).wait_send()

    @pl.when(gx == source)
    def _():
        for o in range(1, count_y):
            if pieces == count_y:
                first(o).wait_send()
                second(o).wait_send()
            else:
                pl.when(span[o] < pieces)(lambda o=o: first(o).wait_send())
                pl.when(gy < pieces)(lambda o=o: second(o).wait_send())
        for o in range(1, count_x):
            for k in range(pieces):
                third(o, k).wait_send()


def fringe_at(gx, x, count_x, cells_x):
    x_glob = (gx * cells_x + x).astype(jnp.float32)
    return fringe_base + fringe_ramp * (x_glob + 0.5) * (1.0 / (count_x * cells_x))


def finish(
    count_x,
    core_ref,
    spread_in,
    inflow_ref,
    force_in,
    rate_ref,
    spread_ref,
    force_ref,
    rate,
    sems,
    rate_sem,
):
    comps, cells_x, levels, cells_y = rate.shape
    gx = lax.axis_index("gx")
    others = [
        pltpu.make_async_copy(spread_in, spread_ref, sems.at[0]),
        pltpu.make_async_copy(force_in, force_ref, sems.at[1]),
    ]
    for copy in others:
        copy.start()

    def out(x):
        return pltpu.make_async_copy(rate.at[:, x], rate_ref.at[:, x], rate_sem.at[x])

    for x in range(cells_x):
        fringe = fringe_at(gx, x, count_x, cells_x)
        for c in range(comps):
            rate[c, x] = core_ref[c, x] + fringe * inflow_ref[c]
        out(x).start()
    for x in range(cells_x):
        out(x).wait()
    for copy in others:
        copy.wait()


def local(velocity_section, point_owner, point_cell, blade_coef, recycle_map):
    comps, cells_x, levels, cells_y = velocity_section.shape
    pts = point_owner.shape[1]
    padded_pts = -(-pts // LANES) * LANES
    count_x, count_y = lax.axis_size("gx"), lax.axis_size("gy")
    pieces = min(count_y, levels // TILE)
    depth = levels // pieces
    vmem = pl.BlockSpec(memory_space=pltpu.VMEM)
    hbm = pl.BlockSpec(memory_space=pltpu.HBM)
    f32 = jnp.float32
    whole = jax.ShapeDtypeStruct(velocity_section.shape, f32)
    at_points = jax.ShapeDtypeStruct((comps, 1, pts), f32)
    dma = pltpu.SemaphoreType.DMA
    core, spread, inflow, force = pl.pallas_call(
        functools.partial(evolve, count_x, count_y),
        out_shape=(
            whole,
            whole,
            jax.ShapeDtypeStruct((comps, levels, cells_y), f32),
            at_points,
        ),
        in_specs=[hbm] * 5,
        out_specs=(vmem,) * 4,
        scratch_shapes=[
            pltpu.VMEM((comps, cells_x + 2, levels, cells_y), f32),
            pltpu.VMEM(point_owner.shape, jnp.int32),
            pltpu.VMEM((3, 1, pts), jnp.int32),
            pltpu.VMEM(blade_coef.shape, f32),
            pltpu.SMEM(recycle_map.shape, jnp.int32),
            pltpu.VMEM((TILE, padded_pts), jnp.int32),
            pltpu.VMEM((TILE, padded_pts), f32),
            pltpu.VMEM((levels, LANES), f32),
            pltpu.VMEM((2, levels, LANES), f32),
            pltpu.VMEM((count_y, comps, depth, cells_y), f32),
            pltpu.VMEM((count_y, comps, depth, cells_y), f32),
            pltpu.VMEM((count_y, TILE, padded_pts), f32),
            dma((5,)),
            dma((2,)),
            dma((2,)),
            dma((2,)),
            dma((2,)),
            dma((count_y,)),
            dma((count_y,)),
            dma((count_y,)),
            dma((count_y,)),
            dma((count_y,)),
            dma((count_y,)),
            dma((count_x, pieces)),
            dma((pieces,)),
        ],
        compiler_params=pltpu.CompilerParams(
            collective_id=0, has_side_effects=True, vmem_limit_bytes=32 * 1024 * 1024
        ),
        name="evolve",
    )(
        velocity_section,
        point_owner,
        point_cell.transpose(1, 0, 2),
        blade_coef,
        recycle_map,
    )
    rate, spread, force = pl.pallas_call(
        functools.partial(finish, count_x),
        out_shape=(whole, whole, at_points),
        in_specs=[vmem] * 4,
        out_specs=(hbm,) * 3,
        scratch_shapes=[
            pltpu.VMEM(velocity_section.shape, f32),
            dma((2,)),
            dma((cells_x,)),
        ],
        compiler_params=pltpu.CompilerParams(vmem_limit_bytes=16 * 1024 * 1024),
        name="finish",
    )(core, spread, inflow, force)
    return rate, spread, force.transpose(1, 0, 2)


def solution(mesh):
    placed = (P(None, "gx", None, "gy"), P("gx", None), P("gx", None, None), P("gx", None), P())
    return jax.shard_map(
        local,
        mesh=mesh,
        in_specs=placed,
        out_specs=(P(None, "gx", None, "gy"), P(None, "gx", None, "gy"), P("gx", None, None)),
        check_vma=False,
    )
```

time: 28 us -> 25.4 us (0.907)
  the two profiles are of different devices: /device:TPU:0 before, /device:TPU:3 now
where the time goes in v2:
time: 25.4 us; the launch traced here: 25.2 us
  Pallas kernels  20.5 us (81%)
  local copies, waits for them, and re-layouts  4.1 us (16%)
  between operations  0.65 us (3%)
    pallas_call x1, Pallas kernels, local(): pl.pallas_call(functools.partial(evolve, count_x, count_y), out_shape=(wh...  18.6 us
    unnamed x10, local copies, waits for them, and re-layouts  4.1 us
    pallas_call x1, Pallas kernels, local(): pl.pallas_call(functools.partial(finish, count_x), out_shape=(whole, whol...  1.83 us

profile of v2, /device:TPU:3, one launch (start us, length us, event | category | flops | bytes accessed | tf_op | source)
XLA Modules:
  0.0 25.2 jit_solution(560718753200383670)
XLA Ops:
  0.6 0.0 copy-start
  0.6 1.4 %copy-done = f32[3,16,64,128]{3,2,1,0:T(8,128)S(1)} copy-done((f32[3,16,64,128]{3,2,1,0:T(8,128)S(1)}, f32[3,16,64,128]{3,2,1,0:T(8,128)}, u32[]{:S(2)}) %copy-start) | copy-done | bytes 1572888
  2.0 0.0 copy-start.1
  2.0 0.7 %copy-done.1 = s32[1,3,240]{2,0,1:T(1,128)S(1)} copy-done((s32[1,3,240]{2,0,1:T(1,128)S(1)}, s32[1,3,240]{2,0,1:T(1,128)}, u32[]{:S(2)}) %copy-start.1) | copy-done | bytes 2904
  2.7 0.0 copy-start.2
  2.7 0.7 %copy-done.2 = s32[1,240]{1,0:T(1,128)S(1)} copy-done((s32[1,240]{1,0:T(1,128)S(1)}, s32[1,240]{1,0:T(1,128)}, u32[]{:S(2)}) %copy-start.2) | copy-done | bytes 984
  3.4 0.0 copy-start.3
  3.4 0.7 %copy-done.3 = f32[1,240]{1,0:T(1,128)S(1)} copy-done((f32[1,240]{1,0:T(1,128)S(1)}, f32[1,240]{1,0:T(1,128)}, u32[]{:S(2)}) %copy-start.3) | copy-done | bytes 984
  4.1 0.0 copy-start.4
  4.1 0.7 %copy-done.4 = s32[8]{0:T(128)S(1)} copy-done((s32[8]{0:T(128)S(1)}, s32[8]{0:T(128)}, u32[]{:S(2)}) %copy-start.4) | copy-done | bytes 56
  4.7 18.6 %evolve.1 = (f32[3,16,64,128]{3,2,1,0:T(8,128)S(1)}, f32[3,16,64,128]{3,2,1,0:T(8,128)S(1)}, f32[3,64,128]{2,1,0:T(8,128)S(1)}, f32[3,1,240]{2,1,0:T(1,128)S(1)}) custom-call(f32[3,16,64,128]{3,2,1,0:T(8,128)S(1)} %copy-done, s32[1,240]{1,0:T(1,128)S(1)} %copy-done.2, s32[3,1,240]{2,1,0:T(1,128)S(1)} %bitcast.2, f32[1,240]{1,0:T(1,128)S(1)} %copy-done.3, ...), custom_call_target="tpu_custom_call" | custom-call | tf_op jit(solution)/shard_map/evolve/pallas_call | solution.py:444
  23.4 1.8 %finish.1 = (f32[3,16,64,128]{3,2,1,0:T(8,128)}, f32[3,16,64,128]{3,2,1,0:T(8,128)}, f32[3,1,240]{2,1,0:T(1,128)}) custom-call(f32[3,16,64,128]{3,2,1,0:T(8,128)S(1)} %get-tuple-element.10.core_ref, f32[3,16,64,128]{3,2,1,0:T(8,128)S(1)} %get-tuple-element.11.spread_in, f32[3,64,128]{2,1,0:T(8,128)S(1)} %get-tuple-element.12.inflow_ref, ...), custom_call_target="tpu_custom_call" | custom-call | tf_op jit(solution)/shard_map/finish/pallas_call | solution.py:492
Async XLA Ops:
  0.6 1.4 %copy-start = (f32[3,16,64,128]{3,2,1,0:T(8,128)S(1)}, f32[3,16,64,128]{3,2,1,0:T(8,128)}, u32[]{:S(2)}) copy-start(f32[3,16,64,128]{3,2,1,0:T(8,128)} %u_ref.1) | copy-start | bytes 4718596
  2.0 0.7 %copy-start.1 = (s32[1,3,240]{2,0,1:T(1,128)S(1)}, s32[1,3,240]{2,0,1:T(1,128)}, u32[]{:S(2)}) copy-start(s32[1,3,240]{2,0,1:T(1,128)} %param.7) | copy-start | bytes 8644
  2.7 0.7 %copy-start.2 = (s32[1,240]{1,0:T(1,128)S(1)}, s32[1,240]{1,0:T(1,128)}, u32[]{:S(2)}) copy-start(s32[1,240]{1,0:T(1,128)} %owner_ref.1) | copy-start | bytes 2884
  3.4 0.7 %copy-start.3 = (f32[1,240]{1,0:T(1,128)S(1)}, f32[1,240]{1,0:T(1,128)}, u32[]{:S(2)}) copy-start(f32[1,240]{1,0:T(1,128)} %gain_ref.1) | copy-start | bytes 2884
  4.1 0.7 %copy-start.4 = (s32[8]{0:T(128)S(1)}, s32[8]{0:T(128)}, u32[]{:S(2)}) copy-start(s32[8]{0:T(128)} %map_ref.1) | copy-start | bytes 100

commit v3 on v2

--- a/solution.py
+++ b/solution.py
@@ -65,8 +65,6 @@
     p1_recv,
     p2_send,
     p2_recv,
-    p3_send,
-    p3_recv,
 ):
     comps, cells_x, levels, cells_y = u_ref.shape
     pts = owner_ref.shape[1]
@@ -94,10 +92,28 @@
         return pl.ds(pl.multiple_of(k * depth, depth), depth)
 
     barrier = pltpu.get_barrier_semaphore()
+
+    def greet(x, y):
+        pl.semaphore_signal(barrier, inc=1, device_id=(x, y), device_id_type=MESH)
+
+    ahead = (gx < count_x - 1) & (gx + 1 != source)
+    behind = (gx > 0) & (gx - 1 != source)
     for o in range(1, count_y):
-        pl.semaphore_signal(barrier, inc=1, device_id=(gx, span[o]), device_id_type=MESH)
-    for o in range(1, count_x):
-        pl.semaphore_signal(barrier, inc=1, device_id=(stream[o], gy), device_id_type=MESH)
+        greet(gx, span[o])
+
+    @pl.when(gx == source)
+    def _():
+        for x in range(1, count_x):
+            for o in range(count_y):
+                greet(stream[x], span[o])
+
+    @pl.when(gx != source)
+    def _():
+        for o in range(count_y):
+            greet(source, span[o])
+        pl.when(ahead)(lambda: greet(stream[1], gy))
+        pl.when(behind)(lambda: greet(stream[count_x - 1], gy))
+
     fetches = [
         pltpu.make_async_copy(src, dst, in_sem.at[n])
         for n, (src, dst) in enumerate(
@@ -112,7 +128,16 @@
     ]
     for fetch in fetches:
         fetch.start()
-    pl.semaphore_wait(barrier, count_y + count_x - 2)
+
+    @pl.when(gx == source)
+    def _():
+        pl.semaphore_wait(barrier, count_x * count_y - 1)
+
+    @pl.when(gx != source)
+    def _():
+        beside = ahead.astype(jnp.int32) + behind.astype(jnp.int32)
+        pl.semaphore_wait(barrier, 2 * count_y - 1 + beside)
+
 
     def first(o):
         return remote(
@@ -160,14 +185,18 @@
     right.start()
     left.start()
 
-    def second(o):
+    def second(x, o):
         return remote(
             picked.at[span[o]],
             inflow_ref.at[:, rows(gy)],
-            p2_send.at[o],
+            p2_send.at[x, o],
             p2_recv.at[gy],
+            x=stream[x],
             y=span[o],
         )
+
+    others = [(x, o) for o in range(count_y) for x in range(1, count_x)]
+    others += [(0, o) for o in range(1, count_y)]
 
     def second_leg():
         held[gy] = cells[:, 1, rows(gy), :]
@@ -177,16 +206,9 @@
             ).wait_recv()
         for j in range(count_y):
             picked[j] = held[order[j]]
-        for o in range(1, count_y):
-            second(o).start()
+        for x, o in others:
+            second(x, o).start()
         inflow_ref[:, rows(gy), :] = picked[gy]
-
-    @pl.when(gx == source)
-    def _():
-        if pieces == count_y:
-            second_leg()
-        else:
-            pl.when(gy < pieces)(second_leg)
 
     points[...] = jnp.zeros_like(points)
     gains[...] = jnp.zeros_like(gains)
@@ -233,38 +255,12 @@
     for o in range(1, count_y):
         share(o).start()
 
-    def third(o, k):
-        return remote(
-            inflow_ref.at[:, rows(k)],
-            inflow_ref.at[:, rows(k)],
-            p3_send.at[o, k],
-            p3_recv.at[k],
-            x=stream[o],
-        )
-
-    def forward(q):
-        k = lax.rem(gy + count_y - q, count_y)
-
-        def arrived():
-            remote(
-                picked.at[0], inflow_ref.at[:, rows(k)], p2_send.at[0], p2_recv.at[k], y=back[1]
-            ).wait_recv()
-
-        def send_on():
-            if q > 0:
-                arrived()
-            for o in range(1, count_x):
-                third(o, k).start()
-
+    @pl.when(gx == source)
+    def _():
         if pieces == count_y:
-            send_on()
+            second_leg()
         else:
-            pl.when(k < pieces)(send_on)
-
-    @pl.when(gx == source)
-    def _():
-        for q in range(count_y):
-            forward(q)
+            pl.when(gy < pieces)(second_leg)
 
     for side in range(2):
         remote(edges, got_edges.at[side], y_send.at[side], y_recv.at[side], y=span[1]).wait_recv()
@@ -342,25 +338,35 @@
     weight_y = kernel_weight(distance.astype(jnp.float32)).astype(jnp.bfloat16)
     point_x = points[3:4, :]
 
-    def spread(x):
-        weight_x = kernel_weight((x - point_x).astype(jnp.float32))
-        weighted = jnp.concatenate(
-            [((forces[c] * weight_x) * weight_z).astype(jnp.bfloat16) for c in range(comps)], 0
-        )
-        spread_ref[:, x] = lax.dot_general(
-            weighted, weight_y, (((1,), (1,)), ((), ())), preferred_element_type=jnp.float32
-        ).reshape(comps, levels, cells_y)
-
-    lax.fori_loop(0, cells_x, lambda x, carry: (spread(x), carry)[1], 0)
+    group = 4
+
+    def spread(step):
+        weighted = []
+        for x in range(group):
+            weight_x = kernel_weight((step * group + x - point_x).astype(jnp.float32))
+            for c in range(comps):
+                weighted.append(((forces[c] * weight_x) * weight_z).astype(jnp.bfloat16))
+        summed = lax.dot_general(
+            jnp.concatenate(weighted, 0),
+            weight_y,
+            (((1,), (1,)), ((), ())),
+            preferred_element_type=jnp.float32,
+        ).reshape(group, comps, levels, cells_y)
+        for x in range(group):
+            spread_ref[:, step * group + x] = summed[x]
+
+    lax.fori_loop(0, cells_x // group, lambda x, carry: (spread(x), carry)[1], 0)
 
     pl.when(gx > 0)(lambda: up.wait_recv())
     pl.when(gx < count_x - 1)(lambda: down.wait_recv())
     planes(cells_x - 1, cells_x)
 
-    @pl.when(gx != source)
-    def _():
-        for k in range(pieces):
-            third(1, k).wait_recv()
+    for k in range(pieces):
+        landing = inflow_ref.at[:, pl.ds(k * depth, depth)]
+
+        @pl.when((gx != source) | (gy != k))
+        def _(k=k, landing=landing):
+            remote(picked.at[0], landing, p2_send.at[0, 0], p2_recv.at[k], y=back[1]).wait_recv()
 
     @pl.when(gx == 0)
     def _():
@@ -378,13 +384,13 @@
         for o in range(1, count_y):
             if pieces == count_y:
                 first(o).wait_send()
-                second(o).wait_send()
             else:
                 pl.when(span[o] < pieces)(lambda o=o: first(o).wait_send())
-                pl.when(gy < pieces)(lambda o=o: second(o).wait_send())
-        for o in range(1, count_x):
-            for k in range(pieces):
-                third(o, k).wait_send()
+        for x, o in others:
+            if pieces == count_y:
+                second(x, o).wait_send()
+            else:
+                pl.when(gy < pieces)(lambda x=x, o=o: second(x, o).wait_send())
 
 
 def fringe_at(gx, x, count_x, cells_x):
@@ -473,9 +479,7 @@
             dma((count_y,)),
             dma((count_y,)),
             dma((count_y,)),
-            dma((count_y,)),
-            dma((count_y,)),
-            dma((count_x, pieces)),
+            dma((count_x, count_y)),
             dma((pieces,)),
         ],
         compiler_params=pltpu.CompilerParams(
@@ -483,11 +487,16 @@
         ),
         name="evolve",
     )(
-        velocity_section,
-        point_owner,
-        point_cell.transpose(1, 0, 2),
-        blade_coef,
-        recycle_map,
+        *(
+            pltpu.with_memory_space_constraint(operand, pltpu.HBM)
+            for operand in (
+                velocity_section,
+                point_owner,
+                point_cell.transpose(1, 0, 2),
+                blade_coef,
+                recycle_map,
+            )
+        )
     )
     rate, spread, force = pl.pallas_call(
         functools.partial(finish, count_x),

time: 25.4 us -> 18.4 us (0.72)
  the two profiles are of different devices: /device:TPU:3 before, /device:TPU:0 now
where the time goes in v3:
time: 18.4 us; the launch traced here: 18.2 us
  Pallas kernels  17.5 us (95%)
  between operations  0.64 us (3%)
    pallas_call x1, Pallas kernels, local(): pl.pallas_call(functools.partial(evolve, count_x, count_y), out_shape=(wh...  15.7 us
    pallas_call x1, Pallas kernels, local(): pl.pallas_call(functools.partial(finish, count_x), out_shape=(whole, whol...  1.83 us

profile of v3, /device:TPU:0, one launch (start us, length us, event | category | flops | bytes accessed | tf_op | source)
XLA Modules:
  0.0 18.2 jit_solution(17367602222883158552)
XLA Ops:
  0.6 15.7 %evolve.1 = (f32[3,16,64,128]{3,2,1,0:T(8,128)S(1)}, f32[3,16,64,128]{3,2,1,0:T(8,128)S(1)}, f32[3,64,128]{2,1,0:T(8,128)S(1)}, f32[3,1,240]{2,1,0:T(1,128)S(1)}) custom-call(f32[3,16,64,128]{3,2,1,0:T(8,128)} %u_ref.1, s32[1,240]{1,0:T(1,128)} %owner_ref.1, s32[3,1,240]{2,1,0:T(1,128)} %bitcast.2, f32[1,240]{1,0:T(1,128)} %gain_ref.1, s32[8]{0:T(128)} %map_ref.1), custom_call_target="tpu_custom_call" | custom-call | tf_op jit(solution)/shard_map/evolve/pallas_call | solution.py:450
  16.3 1.8 %finish.1 = (f32[3,16,64,128]{3,2,1,0:T(8,128)}, f32[3,16,64,128]{3,2,1,0:T(8,128)}, f32[3,1,240]{2,1,0:T(1,128)}) custom-call(f32[3,16,64,128]{3,2,1,0:T(8,128)S(1)} %get-tuple-element.10.core_ref, f32[3,16,64,128]{3,2,1,0:T(8,128)S(1)} %get-tuple-element.11.spread_in, f32[3,64,128]{2,1,0:T(8,128)S(1)} %get-tuple-element.12.inflow_ref, ...), custom_call_target="tpu_custom_call" | custom-call | tf_op jit(solution)/shard_map/finish/pallas_call | solution.py:501

commit v4 on v3

--- a/solution.py
+++ b/solution.py
@@ -49,7 +49,11 @@
     order,
     points,
     gains,
+    near_x,
+    near_y,
+    near_z,
     edges,
+    sides,
     got_edges,
     held,
     picked,
@@ -91,6 +95,9 @@
     def rows(k):
         return pl.ds(pl.multiple_of(k * depth, depth), depth)
 
+    def inner_rows(k):
+        return pl.ds(pl.multiple_of(k * depth, depth) + TILE, depth)
+
     barrier = pltpu.get_barrier_semaphore()
 
     def greet(x, y):
@@ -114,11 +121,12 @@
         pl.when(ahead)(lambda: greet(stream[1], gy))
         pl.when(behind)(lambda: greet(stream[count_x - 1], gy))
 
+    inner = pl.ds(TILE, levels)
     fetches = [
         pltpu.make_async_copy(src, dst, in_sem.at[n])
         for n, (src, dst) in enumerate(
             [
-                (u_ref, cells.at[:, pl.ds(1, cells_x)]),
+                (u_ref, cells.at[:, pl.ds(1, cells_x), inner]),
                 (owner_ref, owner_in),
                 (cell_ref, cell_in),
                 (gain_ref, gain_in),
@@ -139,9 +147,12 @@
         pl.semaphore_wait(barrier, 2 * count_y - 1 + beside)
 
 
+    for fetch in fetches:
+        fetch.wait()
+
     def first(o):
         return remote(
-            u_ref.at[:, 0, rows(span[o])], held.at[gy], p1_send.at[o], p1_recv.at[gy], y=span[o]
+            cells.at[:, 1, inner_rows(span[o])], held.at[gy], p1_send.at[o], p1_recv.at[gy], y=span[o]
         )
 
     @pl.when(gx == source)
@@ -153,11 +164,11 @@
                 pl.when(span[o] < pieces)(lambda o=o: first(o).start())
 
     up = remote(
-        u_ref.at[:, cells_x - 1], cells.at[:, 0], x_send.at[0], x_recv.at[0], x=stream[1]
+        u_ref.at[:, cells_x - 1], cells.at[:, 0, inner], x_send.at[0], x_recv.at[0], x=stream[1]
     )
     down = remote(
         u_ref.at[:, 0],
-        cells.at[:, cells_x + 1],
+        cells.at[:, cells_x + 1, inner],
         x_send.at[1],
         x_recv.at[1],
         x=stream[count_x - 1],
@@ -165,12 +176,12 @@
     pl.when(gx < count_x - 1)(lambda: up.start())
     pl.when(gx > 0)(lambda: down.start())
 
-    for fetch in fetches:
-        fetch.wait()
-
     @pl.when(gx == count_x - 1)
     def _():
-        cells[:, cells_x + 1] = cells[:, cells_x]
+        cells[:, cells_x + 1, inner] = cells[:, cells_x, inner]
+
+    cells[:, :, 0:TILE] = jnp.zeros((comps, cells_x + 2, TILE, cells_y), jnp.float32)
+    cells[:, :, TILE + levels :] = jnp.zeros((comps, cells_x + 2, TILE, cells_y), jnp.float32)
 
     lane = lax.broadcasted_iota(jnp.int32, (levels, LANES), 1)
     packed = jnp.zeros((levels, LANES), jnp.float32)
@@ -178,10 +189,16 @@
     for c in range(comps):
         for x in range(cells_x):
             n = c * cells_x + x
-            packed = jnp.where(slot == n, pltpu.roll(cells[c, x + 1], 2 * n, 1), packed)
-    edges[...] = packed
-    right = remote(edges, got_edges.at[0], y_send.at[0], y_recv.at[0], y=span[1])
-    left = remote(edges, got_edges.at[1], y_send.at[1], y_recv.at[1], y=span[count_y - 1])
+            packed = jnp.where(slot == n, pltpu.roll(cells[c, x + 1, inner], 2 * n, 1), packed)
+    even = lax.rem(lane, 2) == 0
+    upper, lower = packed[0 : levels // 2], packed[levels // 2 :]
+    even_half = even[0 : levels // 2]
+    sides[0] = jnp.where(even_half, pltpu.roll(lower, 1, 1), upper)
+    sides[1] = jnp.where(even_half, upper, pltpu.roll(lower, LANES - 1, 1))
+    right = remote(sides.at[0], got_edges.at[0], y_send.at[0], y_recv.at[0], y=span[1])
+    left = remote(
+        sides.at[1], got_edges.at[1], y_send.at[1], y_recv.at[1], y=span[count_y - 1]
+    )
     right.start()
     left.start()
 
@@ -199,7 +216,7 @@
     others += [(0, o) for o in range(1, count_y)]
 
     def second_leg():
-        held[gy] = cells[:, 1, rows(gy), :]
+        held[gy] = cells[:, 1, pl.ds(pl.multiple_of(gy * depth, depth) + TILE, depth), :]
         for o in range(1, count_y):
             remote(
                 held.at[back[o]], held.at[back[o]], p1_send.at[o], p1_recv.at[back[o]], y=back[o]
@@ -238,16 +255,21 @@
         axis=1,
     )
     at_points = jnp.zeros((padded_pts, LANES), jnp.float32)
+    point = lax.broadcasted_iota(jnp.int32, (padded_pts, LANES), 0)
+    part_row = (lax.div(point, LANES) * comps).astype(jnp.float32)
     for c in range(comps):
-        field = cells[c, 1 : cells_x + 1].reshape(cells_x * levels, cells_y)
+        field = cells[c, 1 : cells_x + 1, TILE : TILE + levels].reshape(cells_x * levels, cells_y)
         total = jnp.zeros((padded_pts, LANES), jnp.float32)
         for _ in range(3):
             part = field.astype(jnp.bfloat16)
             total = total + jnp.dot(chosen, part, preferred_element_type=jnp.float32)
             field = field - part.astype(jnp.float32)
         column = jnp.sum(jnp.where(mine, total, 0.0), axis=1, keepdims=True)
-        at_points = jnp.where(lanes == float(c), column, at_points)
-    parts[gy] = at_points.T[0:TILE]
+        at_points = jnp.where(lanes == part_row + float(c), column, at_points)
+    folded = at_points[0:LANES]
+    for h in range(1, padded_pts // LANES):
+        folded = folded + at_points[h * LANES : (h + 1) * LANES]
+    parts[gy] = folded.T[0:TILE]
 
     def share(o):
         return remote(parts.at[gy], parts.at[gy], v_send.at[o], v_recv.at[gy], y=span[o])
@@ -262,47 +284,60 @@
         else:
             pl.when(gy < pieces)(second_leg)
 
+    deep = lax.broadcasted_iota(jnp.int32, (cells_x, padded_pts), 0)
+    near_x[...] = kernel_weight((deep - points[3:4, :]).astype(jnp.float32))
+    level = lax.broadcasted_iota(jnp.int32, (levels, padded_pts), 0)
+    near_z[...] = kernel_weight((level - points[5:6, :]).astype(jnp.float32))
+    span_total = count_y * cells_y
+    y_cell = lax.broadcasted_iota(jnp.int32, (cells_y, padded_pts), 0) + gy * cells_y
+    distance = y_cell - points[4:5, :]
+    distance = jnp.where(distance >= span_total // 2, distance - span_total, distance)
+    distance = jnp.where(distance < -(span_total // 2), distance + span_total, distance)
+    near_y[...] = kernel_weight(distance.astype(jnp.float32)).astype(jnp.bfloat16)
+
     for side in range(2):
-        remote(edges, got_edges.at[side], y_send.at[side], y_recv.at[side], y=span[1]).wait_recv()
-    right.wait_send()
-    left.wait_send()
-    even = lax.rem(lane, 2) == 0
-    edges[...] = jnp.where(
-        even, pltpu.roll(got_edges[0], 1, 1), pltpu.roll(got_edges[1], LANES - 1, 1)
-    )
-
-    deep = lax.broadcasted_iota(jnp.int32, (levels, cells_y), 0)
+        remote(
+            sides.at[side], got_edges.at[side], y_send.at[side], y_recv.at[side], y=span[1]
+        ).wait_recv()
+    from_left, from_right = got_edges[0], got_edges[1]
+    edges[0 : levels // 2] = jnp.where(
+        even_half, pltpu.roll(from_left, 1, 1), pltpu.roll(from_right, LANES - 1, 1)
+    )
+    edges[levels // 2 :] = jnp.where(even_half, from_left, from_right)
 
     def tendency(x):
-        center, grads, sums = [], [[], [], []], []
+        half, grads, sums, drag = [], [[], [], []], [], []
+        fringe = fringe_at(gx, x, count_x, cells_x)
         for c in range(comps):
-            here, plus, minus = cells[c, x + 1], cells[c, x + 2], cells[c, x]
+            here = cells[c, x + 1, inner]
+            plus, minus = cells[c, x + 2, inner], cells[c, x, inner]
+            z_plus = cells[c, x + 1, TILE + 1 : TILE + 1 + levels]
+            z_minus = cells[c, x + 1, TILE - 1 : TILE - 1 + levels]
             n = 2 * (c * cells_x + x)
             side = pltpu.roll(edges[...], lax.rem(LANES - n, LANES), 1)
             y_minus = jnp.where(lane == 0, side, pltpu.roll(here, 1, 1))
             y_plus = jnp.where(lane == cells_y - 1, side, pltpu.roll(here, cells_y - 1, 1))
-            z_minus = jnp.where(deep == 0, 0.0, pltpu.roll(here, 1, 0))
-            z_plus = jnp.where(deep == levels - 1, 0.0, pltpu.roll(here, levels - 1, 0))
-            center.append(here)
-            grads[0].append((plus - minus) * 0.5)
-            grads[1].append((y_plus - y_minus) * 0.5)
-            grads[2].append((z_plus - z_minus) * 0.5)
-            sums.append(plus + minus + y_plus + y_minus + z_plus + z_minus - 6.0 * here)
+            half.append(0.5 * here)
+            grads[0].append(plus - minus)
+            grads[1].append(y_plus - y_minus)
+            grads[2].append(z_plus - z_minus)
+            sums.append((plus + minus) + (y_plus + y_minus) + (z_plus + z_minus) - 6.0 * here)
+            drag.append(fringe * here)
         diagonal = grads[0][0] * grads[0][0] + grads[1][1] * grads[1][1] + grads[2][2] * grads[2][2]
         s01 = grads[0][1] + grads[1][0]
         s02 = grads[0][2] + grads[2][0]
         s12 = grads[1][2] + grads[2][1]
-        twice = 2.0 * diagonal + (s01 * s01 + s02 * s02 + s12 * s12)
-        eddy = viscosity + smag_sq * jnp.sqrt(twice)
-        fringe = fringe_at(gx, x, count_x, cells_x)
+        twice = (diagonal + diagonal) + (s01 * s01 + s02 * s02 + s12 * s12)
+        eddy = viscosity + (0.5 * smag_sq) * jnp.sqrt(twice)
         for c in range(comps):
-            advect = center[0] * grads[0][c] + center[1] * grads[1][c] + center[2] * grads[2][c]
-            core_ref[c, x] = eddy * sums[c] - advect - fringe * center[c]
+            advect = half[0] * grads[0][c] + half[1] * grads[1][c] + half[2] * grads[2][c]
+            core_ref[c, x] = eddy * sums[c] - (advect + drag[c])
 
     def planes(low, high):
         lax.fori_loop(low, high, lambda x, carry: (tendency(x), carry)[1], 0)
 
-    planes(1, cells_x - 1)
+    early = cells_x // 2 - 1
+    planes(1, early)
 
     for o in range(1, count_y):
         remote(
@@ -312,7 +347,12 @@
     for j in range(1, count_y):
         values = values + parts[j]
     gain = gains[0:1, :]
-    at = [values[c : c + 1] for c in range(comps)]
+    at = [
+        jnp.concatenate(
+            [values[h * comps + c : h * comps + c + 1] for h in range(padded_pts // LANES)], 1
+        )
+        for c in range(comps)
+    ]
     row = lax.broadcasted_iota(jnp.int32, (1, padded_pts), 1)
     axial = jnp.zeros((1, padded_pts), jnp.float32)
     for t in range(pts // per_turb):
@@ -328,34 +368,29 @@
         forces.append(-force_gain * gain * drive)
         force_ref[c] = forces[c][:, 0:pts]
 
-    level = lax.broadcasted_iota(jnp.int32, (levels, padded_pts), 0)
-    weight_z = kernel_weight((level - points[5:6, :]).astype(jnp.float32))
-    span_total = count_y * cells_y
-    y_cell = lax.broadcasted_iota(jnp.int32, (cells_y, padded_pts), 0) + gy * cells_y
-    distance = y_cell - points[4:5, :]
-    distance = jnp.where(distance >= span_total // 2, distance - span_total, distance)
-    distance = jnp.where(distance < -(span_total // 2), distance + span_total, distance)
-    weight_y = kernel_weight(distance.astype(jnp.float32)).astype(jnp.bfloat16)
-    point_x = points[3:4, :]
-
-    group = 4
+    group = 2
 
     def spread(step):
         weighted = []
         for x in range(group):
-            weight_x = kernel_weight((step * group + x - point_x).astype(jnp.float32))
+            weight_x = near_x[pl.ds(step * group + x, 1), :]
             for c in range(comps):
-                weighted.append(((forces[c] * weight_x) * weight_z).astype(jnp.bfloat16))
+                weighted.append(((forces[c] * weight_x) * near_z[...]).astype(jnp.bfloat16))
         summed = lax.dot_general(
             jnp.concatenate(weighted, 0),
-            weight_y,
+            near_y[...],
             (((1,), (1,)), ((), ())),
             preferred_element_type=jnp.float32,
         ).reshape(group, comps, levels, cells_y)
         for x in range(group):
             spread_ref[:, step * group + x] = summed[x]
 
-    lax.fori_loop(0, cells_x // group, lambda x, carry: (spread(x), carry)[1], 0)
+    def both(step, carry):
+        spread(step)
+        tendency(early + step)
+        return carry
+
+    lax.fori_loop(0, cells_x // group, both, 0)
 
     pl.when(gx > 0)(lambda: up.wait_recv())
     pl.when(gx < count_x - 1)(lambda: down.wait_recv())
@@ -370,10 +405,12 @@
 
     @pl.when(gx == 0)
     def _():
-        cells[:, 0] = inflow_ref[...]
+        cells[:, 0, inner] = inflow_ref[...]
 
     planes(0, 1)
 
+    right.wait_send()
+    left.wait_send()
     pl.when(gx < count_x - 1)(lambda: up.wait_send())
     pl.when(gx > 0)(lambda: down.wait_send())
     for o in range(1, count_y):
@@ -414,22 +451,22 @@
     comps, cells_x, levels, cells_y = rate.shape
     gx = lax.axis_index("gx")
     others = [
-        pltpu.make_async_copy(spread_in, spread_ref, sems.at[0]),
-        pltpu.make_async_copy(force_in, force_ref, sems.at[1]),
+        pltpu.make_async_copy(spread_in.at[c], spread_ref.at[c], sems.at[c + 1])
+        for c in range(comps)
     ]
+    others.append(pltpu.make_async_copy(force_in, force_ref, sems.at[0]))
     for copy in others:
         copy.start()
 
-    def out(x):
-        return pltpu.make_async_copy(rate.at[:, x], rate_ref.at[:, x], rate_sem.at[x])
-
-    for x in range(cells_x):
-        fringe = fringe_at(gx, x, count_x, cells_x)
-        for c in range(comps):
-            rate[c, x] = core_ref[c, x] + fringe * inflow_ref[c]
-        out(x).start()
-    for x in range(cells_x):
-        out(x).wait()
+    def out(c):
+        return pltpu.make_async_copy(rate.at[c], rate_ref.at[c], rate_sem.at[c])
+
+    for c in range(comps):
+        for x in range(cells_x):
+            rate[c, x] = core_ref[c, x] + fringe_at(gx, x, count_x, cells_x) * inflow_ref[c]
+        out(c).start()
+    for c in range(comps):
+        out(c).wait()
     for copy in others:
         copy.wait()
 
@@ -458,18 +495,22 @@
         in_specs=[hbm] * 5,
         out_specs=(vmem,) * 4,
         scratch_shapes=[
-            pltpu.VMEM((comps, cells_x + 2, levels, cells_y), f32),
+            pltpu.VMEM((comps, cells_x + 2, levels + 2 * TILE, cells_y), f32),
             pltpu.VMEM(point_owner.shape, jnp.int32),
             pltpu.VMEM((3, 1, pts), jnp.int32),
             pltpu.VMEM(blade_coef.shape, f32),
             pltpu.SMEM(recycle_map.shape, jnp.int32),
             pltpu.VMEM((TILE, padded_pts), jnp.int32),
             pltpu.VMEM((TILE, padded_pts), f32),
+            pltpu.VMEM((cells_x, padded_pts), f32),
+            pltpu.VMEM((cells_y, padded_pts), jnp.bfloat16),
+            pltpu.VMEM((levels, padded_pts), f32),
             pltpu.VMEM((levels, LANES), f32),
-            pltpu.VMEM((2, levels, LANES), f32),
+            pltpu.VMEM((2, levels // 2, LANES), f32),
+            pltpu.VMEM((2, levels // 2, LANES), f32),
             pltpu.VMEM((count_y, comps, depth, cells_y), f32),
             pltpu.VMEM((count_y, comps, depth, cells_y), f32),
-            pltpu.VMEM((count_y, TILE, padded_pts), f32),
+            pltpu.VMEM((count_y, TILE, LANES), f32),
             dma((5,)),
             dma((2,)),
             dma((2,)),
@@ -505,8 +546,8 @@
         out_specs=(hbm,) * 3,
         scratch_shapes=[
             pltpu.VMEM(velocity_section.shape, f32),
-            dma((2,)),
-            dma((cells_x,)),
+            dma((comps + 1,)),
+            dma((comps,)),
         ],
         compiler_params=pltpu.CompilerParams(vmem_limit_bytes=16 * 1024 * 1024),
         name="finish",

time: 18.4 us -> 18 us (0.978)
  Pallas kernels: 17.5 us -> 17.2 us
    pallas_call x1, Pallas kernels: 15.7 us -> 15.5 us  [local(): pl.pallas_call(functools.partial(evolve, count_x, count_y), out_shape=(wh...]
where the time goes in v4:
time: 18 us; the launch traced here: 17.9 us
  Pallas kernels  17.2 us (96%)
  between operations  0.64 us (4%)
    pallas_call x1, Pallas kernels, local(): pl.pallas_call(functools.partial(evolve, count_x, count_y), out_shape=(wh...  15.5 us
    pallas_call x1, Pallas kernels, local(): pl.pallas_call(functools.partial(finish, count_x), out_shape=(whole, whol...  1.73 us

profile of v4, /device:TPU:0, one launch (start us, length us, event | category | flops | bytes accessed | tf_op | source)
XLA Modules:
  0.0 17.9 jit_solution(1217120813177197886)
XLA Ops:
  0.6 15.5 %evolve.1 = (f32[3,16,64,128]{3,2,1,0:T(8,128)S(1)}, f32[3,16,64,128]{3,2,1,0:T(8,128)S(1)}, f32[3,64,128]{2,1,0:T(8,128)S(1)}, f32[3,1,240]{2,1,0:T(1,128)S(1)}) custom-call(f32[3,16,64,128]{3,2,1,0:T(8,128)} %u_ref.1, s32[1,240]{1,0:T(1,128)} %owner_ref.1, s32[3,1,240]{2,1,0:T(1,128)} %bitcast.2, f32[1,240]{1,0:T(1,128)} %gain_ref.1, s32[8]{0:T(128)} %map_ref.1), custom_call_target="tpu_custom_call" | custom-call | tf_op jit(solution)/shard_map/evolve/pallas_call | solution.py:487
  16.1 1.7 %finish.1 = (f32[3,16,64,128]{3,2,1,0:T(8,128)}, f32[3,16,64,128]{3,2,1,0:T(8,128)}, f32[3,1,240]{2,1,0:T(1,128)}) custom-call(f32[3,16,64,128]{3,2,1,0:T(8,128)S(1)} %get-tuple-element.10.core_ref, f32[3,16,64,128]{3,2,1,0:T(8,128)S(1)} %get-tuple-element.11.spread_in, f32[3,64,128]{2,1,0:T(8,128)S(1)} %get-tuple-element.12.inflow_ref, ...), custom_call_target="tpu_custom_call" | custom-call | tf_op jit(solution)/shard_map/finish/pallas_call | solution.py:542
